TPU v7x, 512 devices: a whole 4x4x16 slice. The times are simulated.
512 devices in a mesh: dp: 16 (over z), expert: 32 (over y, x, core).
Axes of the slice: x: 4, y: 4, z: 16, core: 2. Of those that a mesh axis runs over, the one named last changes fastest.
Arguments:
- train_x: bfloat16 [65536, 5120], P(('dp', 'expert')), may hold values from -6 to 6
- train_grad: bfloat16 [65536, 6, 1536], P(('dp', 'expert')), may hold values from -0.119628906 to 0.119628906
- train_routes: int32 [65536, 6], P(('dp', 'expert')), may hold values from 0 to 159, all different within a row; in each aligned block of 128 rows (0 to 127, 128 to 255, ...) at most 6 rows name the same one
- train_weight: float32 [65536, 6], P(('dp', 'expert')), may hold values from 0.05 to 1
- train_example: int32 [65536], P(('dp', 'expert')), may hold values from 0 to 3
- probe_x: bfloat16 [1024, 5120], P('dp'), may hold values from -6 to 6
- probe_grad: bfloat16 [1024, 6, 1536], P('dp'), may hold values from -0.119628906 to 0.119628906
- probe_routes: int32 [1024, 6], P('dp'), may hold values from 0 to 159, all different within a row; in each aligned block of 64 rows (0 to 63, 64 to 127, ...) at most 3 rows name the same one
- probe_weight: float32 [1024, 6], P('dp'), may hold values from 0.05 to 1
- probe_example: int32 [1024], P('dp'), may hold values from 0 to 7
Outputs:
- scores: float32 [2048, 128], P(('dp', 'expert'))
Inputs may be any that keep to these rules, and one draw needn't show every extreme that they name: `train_routes`: in the rows of one device no expert is named more than 6 times, a bound that some block reaches. `probe_routes`: in the rows of one index of dp no expert is named more than 3 times, a bound that some block reaches.
All inputs are finite; a program needn't handle non-finite values.
Results may differ from a plain program's by a relative error of at most 0.004.
Values may be sent and summed in bfloat16 or wider, within the bound.
A program may use at most 128 MiB of HBM per device.

v0:
```python
import math

import jax
import jax.numpy as jnp
from jax import lax
from jax.sharding import PartitionSpec as P

EXP_DEV = 5
EX_DEV = 4
PEX_ROW = 8


def slot_table(flat_routes, first_expert, group_size, capacity):
    route_total = flat_routes.shape[0]
    relative = flat_routes - first_expert
    member = relative[:, None] == jnp.arange(group_size, dtype=jnp.int32)[None, :]
    width = math.gcd(route_total, 64)
    blocks = route_total // width
    marks = member.astype(jnp.bfloat16).reshape(blocks, width, group_size)
    lower = (
        jnp.arange(width, dtype=jnp.int32)[:, None] > jnp.arange(width, dtype=jnp.int32)[None, :]
    ).astype(jnp.bfloat16)
    within = jnp.einsum("ij,bjg->big", lower, marks, preferred_element_type=jnp.float32)
    totals = jnp.sum(marks.astype(jnp.float32), axis=1)
    before = jnp.cumsum(totals, axis=0) - totals
    rank_table = (within + before[:, None, :]).reshape(route_total, group_size)
    own_rank = jnp.sum(jnp.where(member, rank_table, 0.0), axis=1).astype(jnp.int32)
    inside = (relative >= 0) & (relative < group_size)
    target = jnp.where(inside, relative * capacity + own_rank, group_size * capacity)
    slot_index = jnp.full((group_size * capacity + 1,), -1, jnp.int32)
    slot_index = slot_index.at[target].set(jnp.arange(route_total, dtype=jnp.int32))
    return slot_index[: group_size * capacity]


def body(
    train_x,
    train_grad,
    train_routes,
    train_weight,
    train_example,
    probe_x,
    probe_grad,
    probe_routes,
    probe_weight,
    probe_example,
):
    tok_rows = train_x.shape[0]
    route_count = train_routes.shape[1]
    probe_rows = probe_x.shape[0]
    dp_count = lax.axis_size("dp")
    expert_count = lax.axis_size("expert")
    experts = EXP_DEV * expert_count
    capacity = max(2, (5 * tok_rows * route_count + 4 * experts - 1) // (4 * experts))
    probe_cap = max(2, (5 * probe_rows * route_count + 4 * experts - 1) // (4 * experts))
    probe_classes = PEX_ROW * dp_count
    dp_index = lax.axis_index("dp")
    column = lax.axis_index("expert")
    train_scaled = (
        (train_weight[:, :, None] * train_grad.astype(jnp.float32))
        .astype(jnp.bfloat16)
        .reshape(tok_rows * route_count, -1)
    )
    home_table = slot_table(train_routes.reshape(-1), 0, experts, capacity)
    home_valid = home_table >= 0
    home_safe = jnp.maximum(home_table, 0)
    home_token = home_safe // route_count
    grad_slots = jnp.where(home_valid[:, None], train_scaled[home_safe], 0).reshape(
        expert_count, EXP_DEV * capacity, -1
    )
    slot_example = jnp.where(home_valid, train_example[home_token], -1)
    probe_scaled = (
        (probe_weight[:, :, None] * probe_grad.astype(jnp.float32))
        .astype(jnp.bfloat16)
        .reshape(probe_rows * route_count, -1)
    )
    near_table = slot_table(probe_routes.reshape(-1), column * EXP_DEV, EXP_DEV, probe_cap)
    near_valid = near_table >= 0
    near_safe = jnp.maximum(near_table, 0)
    probe_owner = dp_index * PEX_ROW + probe_example[near_safe // route_count]
    probe_onehot = (
        (
            (probe_owner[:, None] == jnp.arange(probe_classes, dtype=jnp.int32)[None, :])
            & near_valid[:, None]
        )
        .astype(jnp.bfloat16)
        .reshape(EXP_DEV, probe_cap, probe_classes)
    )
    probe_gsel = jnp.where(near_valid[:, None], probe_scaled[near_safe], 0).reshape(
        EXP_DEV, probe_cap, -1
    )
    feature_slots = jnp.where(home_valid[:, None], train_x[home_token], 0).reshape(
        expert_count, EXP_DEV * capacity, -1
    )
    probe_xsel = jnp.where(near_valid[:, None], probe_x[near_safe // route_count], 0).reshape(
        EXP_DEV, probe_cap, -1
    )
    feature_recv, grad_recv = (
        lax.all_to_all(feature_slots, "expert", split_axis=0, concat_axis=0, tiled=True),
        lax.all_to_all(grad_slots, "expert", split_axis=0, concat_axis=0, tiled=True),
    )
    probe_feat, probe_grads, probe_marks = (
        lax.all_gather(probe_xsel, "dp", axis=1, tiled=True),
        lax.all_gather(probe_gsel, "dp", axis=1, tiled=True),
        lax.all_gather(probe_onehot, "dp", axis=1, tiled=True),
    )
    feature_recv = feature_recv.reshape(expert_count, EXP_DEV, capacity, -1)
    feature_gram = jnp.einsum(
        "skcd,kpd->skcp", feature_recv, probe_feat, preferred_element_type=jnp.float32
    )
    grad_recv = grad_recv.reshape(expert_count, EXP_DEV, capacity, -1)
    grad_gram = jnp.einsum(
        "skcf,kpf->skcp", grad_recv, probe_grads, preferred_element_type=jnp.float32
    )
    pair_values = feature_gram * grad_gram
    per_probe = jnp.einsum(
        "skcp,kpb->skcb",
        pair_values,
        probe_marks.astype(jnp.float32),
        precision=lax.Precision.HIGHEST,
    )
    per_probe = per_probe.reshape(expert_count, EXP_DEV * capacity, probe_classes)
    returned = lax.all_to_all(per_probe, "expert", split_axis=0, concat_axis=0, tiled=True)
    owner_marks = (slot_example[:, None] == jnp.arange(EX_DEV, dtype=jnp.int32)[None, :]).astype(
        jnp.float32
    )
    scores = jnp.einsum(
        "se,sb->eb",
        owner_marks,
        returned.reshape(experts * capacity, probe_classes),
        precision=lax.Precision.HIGHEST,
    )
    return scores


def solution(mesh):
    in_specs = (
        P(("dp", "expert"), None),
        P(("dp", "expert"), None, None),
        P(("dp", "expert"), None),
        P(("dp", "expert"), None),
        P(("dp", "expert")),
        P("dp", None),
        P("dp", None, None),
        P("dp", None),
        P("dp", None),
        P("dp"),
    )
    out_specs = P(("dp", "expert"), None)
    return jax.shard_map(body, mesh=mesh, in_specs=in_specs, out_specs=out_specs, check_vma=False)
```

profile of v0, /device:TPU:1, one launch (start us, length us, event | category | flops | bytes accessed | tf_op | source)
XLA Modules:
  0.0 287.8 jit_solution(2943138931777035645)
XLA Ops:
  6.5 0.8 compare_and_fusion.1
  7.4 0.7 broadcast_multiply_fusion.1
  8.1 0.8 copy.26
  10.4 3.4 %scatter_custom_fusion = s32[961]{0:T(1024)S(1)} fusion(s32[768]{0:T(1024)S(1)} %fusion.24, s32[768]{0:T(1024)S(1)} %iota.57, s32[]{:T(128)} %constant.19.clone.1), kind=kCustom, calls=%fused_computation.66 | custom fusion | bytes 3848 | tf_op jit(solution)/shard_map/scatter | solution.py:31
  13.9 6.2 %gather_fusion = s32[960]{0:T(1024)S(1)} fusion(s32[128]{0:T(128)S(1)} %copy-done.2, s32[1024]{0:T(1024)S(1)} %get-tuple-element.14), kind=kCustom, calls=%fused_computation | custom fusion | bytes 11520 | tf_op jit(solution)/shard_map/gather | solution.py:70
  20.3 2.1 multiply_convert_fusion
  22.4 3.0 %copy.39 = bf16[128,6,1536]{2,1,0:T(8,128)(2,1)} copy(bf16[128,6,1536]{2,0,1:T(8,128)(2,1)S(1)} %multiply_convert_fusion) | data formatting | bytes 4718592 | tf_op jit(solution)/shard_map/convert_element_type | solution.py:60
  25.4 5.0 %reshape.279 = bf16[768,1536]{1,0:T(8,128)(2,1)} reshape(bf16[128,6,1536]{2,1,0:T(8,128)(2,1)} %copy.39) | data formatting | bytes 4718592 | tf_op jit(solution)/shard_map/reshape | solution.py:61
  30.4 9.2 %gather_fusion.5 = bf16[960,1536]{1,0:T(8,128)(2,1)} fusion(bf16[768,1536]{1,0:T(8,128)(2,1)} %reshape.279, s32[1024]{0:T(1024)S(1)} %get-tuple-element.13), kind=kCustom, calls=%fused_computation.5 | custom fusion | bytes 5902080 | tf_op jit(solution)/shard_map/gather | solution.py:67
  39.5 4.5 %gather.35 = bf16[32,30,1536]{2,1,0:T(8,128)(2,1)} reshape(bf16[960,1536]{1,0:T(8,128)(2,1)} %gather_fusion.5) | data formatting | bytes 5898240 | tf_op jit(solution)/shard_map/gather | solution.py:67
  44.0 3.9 %broadcast_select_fusion.1 = bf16[32,30,1536]{2,1,0:T(8,128)(2,1)} fusion(bf16[32,30,1536]{2,1,0:T(8,128)(2,1)} %gather.35, pred[32,30]{1,0:T(8,128)(4,1)S(1)} %ge.41), kind=kLoop, calls=%fused_computation.10 | loop fusion | flops 1474560 | bytes 5899200 | tf_op jit(solution)/shard_map/jit(_where)/select_n | solution.py:67
  47.9 11.3 %all-to-all-start.1 = ((bf16[32,30,1536]{2,1,0:T(8,128)(2,1)}), bf16[32,30,1536]{2,1,0:T(8,128)(2,1)}, u32[]{:S(2)}, u32[]{:S(2)}) async-start(bf16[32,30,1536]{2,1,0:T(8,128)(2,1)} %broadcast_select_fusion.1), calls=%async_computation.1 | async-start | bytes 6291456 | tf_op jit(solution)/shard_map/all_to_all | solution.py:99
  59.2 8.5 %gather_fusion.3 = bf16[960,5120]{1,0:T(8,128)(2,1)} fusion(bf16[128,5120]{1,0:T(8,128)(2,1)S(1)} %copy-done, s32[1024]{0:T(1024)S(1)} %get-tuple-element.14), kind=kCustom, calls=%fused_computation.3 | custom fusion | bytes 19664640 | tf_op jit(solution)/shard_map/gather | solution.py:91
  67.7 10.8 %gather.31 = bf16[32,30,5120]{2,1,0:T(8,128)(2,1)} reshape(bf16[960,5120]{1,0:T(8,128)(2,1)} %gather_fusion.3) | data formatting | bytes 19660800 | tf_op jit(solution)/shard_map/gather | solution.py:91
  78.5 10.0 %broadcast_select_fusion = bf16[32,30,5120]{2,1,0:T(8,128)(2,1)} fusion(bf16[32,30,5120]{2,1,0:T(8,128)(2,1)} %gather.31, pred[32,30]{1,0:T(8,128)(4,1)S(1)} %ge.41), kind=kLoop, calls=%fused_computation.8 | loop fusion | flops 4915200 | bytes 19661760 | tf_op jit(solution)/shard_map/jit(_where)/select_n | solution.py:91
  88.5 10.0 %all-to-all-done.1 = bf16[32,30,1536]{2,1,0:T(8,128)(2,1)} async-done(((bf16[32,30,1536]{2,1,0:T(8,128)(2,1)}), bf16[32,30,1536]{2,1,0:T(8,128)(2,1)}, u32[]{:S(2)}, u32[]{:S(2)}) %all-to-all-start.1) | async-done | bytes 2949152 | tf_op jit(solution)/shard_map/all_to_all | solution.py:99
  98.5 7.4 %all-to-all-start = ((bf16[32,30,5120]{2,1,0:T(8,128)(2,1)}), bf16[32,30,5120]{2,1,0:T(8,128)(2,1)}, u32[]{:S(2)}, u32[]{:S(2)}) async-start(bf16[32,30,5120]{2,1,0:T(8,128)(2,1)} %broadcast_select_fusion), calls=%async_computation | async-start | bytes 20971520 | tf_op jit(solution)/shard_map/all_to_all | solution.py:98
  107.3 3.1 %scatter_custom_fusion.1 = s32[16]{0:T(128)S(1)} fusion(s32[384]{0:T(512)S(1)} %fusion.27, s32[384]{0:T(512)S(1)} %iota.58, s32[]{:T(128)} %constant.19.clone.1), kind=kCustom, calls=%fused_computation.72 | custom fusion | bytes 68 | tf_op jit(solution)/shard_map/scatter | solution.py:31
  110.4 0.6 gather_fusion.2
  111.4 0.8 copy_select_fusion
  112.5 0.7 copy.37
  113.6 0.6 gather_fusion.4
  114.2 0.7 gather_fusion.1
  115.2 29.2 %all_gather.9 = bf16[5,48,128]{2,0,1:T(8,128)(2,1)S(1)} all-gather(bf16[5,3,128]{2,0,1:T(8,128)(2,1)S(1)} %fusion.21), channel_id=1, replica_groups=mesh['dp'=16,'expert'=32] {'dp'}, dimensions={1}, use_global_device_ids=true | all-gather | bytes 65280 | tf_op jit(solution)/shard_map/all_gather | solution.py:104
  144.4 40.9 %all_gather.11 = bf16[5,48,1536]{2,0,1:T(8,128)(2,1)S(1)} all-gather(bf16[5,3,1536]{2,0,1:T(8,128)(2,1)S(1)} %copy_select_fusion.1), channel_id=1, replica_groups=mesh['dp'=16,'expert'=32] {'dp'}, dimensions={1}, use_global_device_ids=true | all-gather | bytes 783360 | tf_op jit(solution)/shard_map/all_gather | solution.py:103
  185.3 5.2 %copy.40 = bf16[32,30,1536]{2,0,1:T(8,128)(2,1)} copy(bf16[32,30,1536]{2,1,0:T(8,128)(2,1)} %all-to-all-done.1) | data formatting | bytes 5898240 | tf_op jit(solution)/shard_map/all_to_all | solution.py:99
  190.6 40.6 %all-to-all-done = bf16[32,30,5120]{2,1,0:T(8,128)(2,1)} async-done(((bf16[32,30,5120]{2,1,0:T(8,128)(2,1)}), bf16[32,30,5120]{2,1,0:T(8,128)(2,1)}, u32[]{:S(2)}, u32[]{:S(2)}) %all-to-all-start) | async-done | bytes 9830432 | tf_op jit(solution)/shard_map/all_to_all | solution.py:98
  231.2 13.1 %copy.34 = bf16[32,30,5120]{2,0,1:T(8,128)(2,1)} copy(bf16[32,30,5120]{2,1,0:T(8,128)(2,1)} %all-to-all-done) | data formatting | bytes 19660800 | tf_op jit(solution)/shard_map/all_to_all | solution.py:98
  244.3 11.4 %fusion = f32[5,48,32,6]{1,2,3,0:T(8,128)S(1)} fusion(bf16[32,5,6,5120]{3,0,2,1:T(8,128)(2,1)} %bitcast.31, bf16[5,48,5120,1]{2,0,1,3:T(8,128)(2,1)} %bitcast.35), kind=kOutput, calls=%fused_computation.11 | convolution fusion | flops 471859200 | bytes 12472320 | tf_op jit(solution)/shard_map/skcd,kpd->skcp/dot_general | solution.py:107
  255.7 1.0 fusion.4
  257.4 22.2 %all_to_all.15 = f32[32,30,128]{2,1,0:T(8,128)S(1)} all-to-all(f32[32,30,128]{2,1,0:T(8,128)S(1)} %copy.43), channel_id=1, replica_groups=mesh['dp'=16,'expert'=32] {'expert'}, dimensions={0} | all-to-all | bytes 983040 | tf_op jit(solution)/shard_map/all_to_all | solution.py:122
  279.7 1.3 fusion.11
  (73 shorter events, 5.1 us)
Async XLA Ops:
  6.5 52.6 %copy-start = (bf16[128,5120]{1,0:T(8,128)(2,1)S(1)}, bf16[128,5120]{1,0:T(8,128)(2,1)}, u32[]{:S(2)}) copy-start(bf16[128,5120]{1,0:T(8,128)(2,1)} %param.10) | copy-start | bytes 3932164
  6.5 7.3 %copy-start.2 = (s32[128]{0:T(128)S(1)}, s32[128]{0:T(128)}, u32[]{:S(2)}) copy-start(s32[128]{0:T(128)} %param.14) | copy-start | bytes 1540
  7.3 12.9 %copy-start.9 = (f32[128,6]{0,1:T(8,128)S(1)}, f32[128,6]{0,1:T(8,128)}, u32[]{:S(2)}) copy-start(f32[128,6]{0,1:T(8,128)} %param.13) | copy-start | bytes 9220
  47.9 50.6 %all-to-all-start.1 = ((bf16[32,30,1536]{2,1,0:T(8,128)(2,1)}), bf16[32,30,1536]{2,1,0:T(8,128)(2,1)}, u32[]{:S(2)}, u32[]{:S(2)}) async-start(bf16[32,30,1536]{2,1,0:T(8,128)(2,1)} %broadcast_select_fusion.1), calls=%async_computation.1 | async-start | bytes 6291456 | tf_op jit(solution)/shard_map/all_to_all | solution.py:99
  88.5 17.5 %copy-start.8 = (s32[64,6]{0,1:T(8,128)S(1)}, s32[64,6]{0,1:T(8,128)}, u32[]{:S(2)}) copy-start(s32[64,6]{0,1:T(8,128)} %param.17) | copy-start | bytes 4612
  88.5 21.9 %copy-start.5 = (bf16[64,5120]{1,0:T(8,128)(2,1)S(1)}, bf16[64,5120]{1,0:T(8,128)(2,1)}, u32[]{:S(2)}) copy-start(bf16[64,5120]{1,0:T(8,128)(2,1)} %param.15) | copy-start | bytes 1966084
  88.5 23.7 %copy-start.7 = (f32[64,6]{0,1:T(8,128)S(1)}, f32[64,6]{0,1:T(8,128)}, u32[]{:S(2)}) copy-start(f32[64,6]{0,1:T(8,128)} %param.18) | copy-start | bytes 4612
  98.5 132.7 %all-to-all-start = ((bf16[32,30,5120]{2,1,0:T(8,128)(2,1)}), bf16[32,30,5120]{2,1,0:T(8,128)(2,1)}, u32[]{:S(2)}, u32[]{:S(2)}) async-start(bf16[32,30,5120]{2,1,0:T(8,128)(2,1)} %broadcast_select_fusion), calls=%async_computation | async-start | bytes 20971520 | tf_op jit(solution)/shard_map/all_to_all | solution.py:98
  105.9 6.3 %copy-start.6 = (bf16[64,6,1536]{2,0,1:T(8,128)(2,1)S(1)}, bf16[64,6,1536]{2,0,1:T(8,128)(2,1)}, u32[]{:S(2)}) copy-start(bf16[64,6,1536]{2,0,1:T(8,128)(2,1)} %param.16) | copy-start | bytes 3538948
  105.9 138.3 %all-gather.2.cloned.1.call-start = ((), (), s32[]{:S(2)}) async-start(), calls=%async_computation.3 | async-start | bytes 4177920 | tf_op jit(solution)/shard_map/all_gather | solution.py:102
  112.5 1.8 copy-start.3
  244.3 11.4 %copy-start.4 = (bf16[32,30,1536]{2,0,1:T(8,128)(2,1)S(1)}, bf16[32,30,1536]{2,0,1:T(8,128)(2,1)}, u32[]{:S(2)}) copy-start(bf16[32,30,1536]{2,0,1:T(8,128)(2,1)} %copy.40) | copy-start | bytes 8847364
  255.7 25.3 %copy-start.1 = (bf16[128,5120]{1,0:T(8,128)(2,1)S(1)}, bf16[128,5120]{1,0:T(8,128)(2,1)}, u32[]{:S(2)}) copy-start(bf16[128,5120]{1,0:T(8,128)(2,1)} %param.10) | copy-start | bytes 3932164
Sparse Core Ops, SparseCore 0:
  112.3 79.6 all-gather.1
where the time goes:
time: 289 us; the launch traced here: 288 us
  blocking collectives  92.3 us (32%)
  local copies, waits for them, and re-layouts  78.2 us (27%)
  waiting for transfers between devices  50.6 us (18%)
  other arithmetic  19.4 us (7%)
  starting transfers between devices  18.8 us (7%)
  matrix products  14.7 us (5%)
  between operations  13.8 us (5%)
    all_gather x1, blocking collectives, body(): lax.all_gather(probe_gsel, 'dp', axis=1, tiled=True)  40.9 us
    all_to_all x1, waiting for transfers between devices, body(): lax.all_to_all(feature_slots, 'expert', split_axis=0, concat_axis=0, tile...  40.6 us
    all_gather x1, blocking collectives, body(): lax.all_gather(probe_onehot, 'dp', axis=1, tiled=True)  29.2 us
    all_to_all x1, blocking collectives, body(): lax.all_to_all(per_probe, 'expert', split_axis=0, concat_axis=0, tiled=True)  22.2 us
    gather x2, local copies, waits for them, and re-layouts, body(): train_x[home_token]  19.3 us
    gather x2, local copies, waits for them, and re-layouts, body(): train_scaled[home_safe]  13.6 us
    all_to_all x1, local copies, waits for them, and re-layouts, body(): lax.all_to_all(feature_slots, 'expert', split_axis=0, concat_axis=0, tile...  13.1 us
    dot_general x1, matrix products, body(): jnp.einsum('skcd,kpd->skcp', feature_recv, probe_feat, preferred_element_...  11.4 us
  transfers between devices with their start and end apart: 3, of which 2 were waited for; matrix products, arithmetic and copies ran while one was open for 20% of the time, Pallas kernels for 0%

commit v1 on v0

v1 whole, which is shorter than its diff:
```python
import jax
import jax.numpy as jnp
from jax import lax
from jax.experimental import pallas as pl
from jax.experimental.pallas import tpu as pltpu
from jax.sharding import PartitionSpec as P

MESH = pl.DeviceIdType.MESH
BF = jnp.bfloat16
F32 = jnp.float32

LANE = 128
TOK = 128
PROW = 64
TOP = 6
D = 5120
FF = 1536
NZ = 16
NR = 4
SLOTS = 8
OWN = 8
PEX_ROW = 8
EX_DEV = 4

XP = D // LANE
GP = FF // LANE
X0 = 1
G0 = X0 + XP
PANELS = G0 + GP * TOP
ALONE = 1 + 8
PART = (PANELS - ALONE) // (2 * NR)
HALF = (PART + 1) // 2


def nt(a, b):
    return lax.dot_general(a, b, (((1,), (1,)), ((), ())), preferred_element_type=F32)


def split(v):
    hi = v.astype(BF)
    return hi, (v - hi.astype(F32)).astype(BF)


def kernel(
    tx_hbm,
    tg_hbm,
    tr_ref,
    tw_ref,
    te_ref,
    px_hbm,
    pg_hbm,
    pr_ref,
    pw_ref,
    pe_ref,
    out_ref,
    slots,
    tx,
    tg,
    rawg,
    ids,
    marks,
    square,
    pmarks,
    xs,
    acc,
    rbuf,
    lsem,
    zs,
    zr,
    rs,
    rr,
    es,
    er,
):
    z = lax.axis_index("dp")
    e = lax.axis_index("expert")
    core = e % 2
    xi = (e // 2) % NR
    yi = e // (2 * NR)

    def at(dz, dx, dy):
        zz = (z + NZ + dz) % NZ
        xx = (xi + NR + dx) % NR
        yy = (yi + NR + dy) % NR
        return (zz, (yy * NR + xx) * 2 + core)

    other = (z, e + 1 - 2 * core)
    up = jnp.where(core == 0, -1, 1)
    znext = at(up, 0, 0)
    sides = ((at(0, 1, 0), at(0, -1, 0)), (at(0, 0, 1), at(0, 0, -1)))
    rank = (xi, yi)
    base = (ALONE, ALONE + NR * PART)
    own = jnp.where(core == 0, OWN, 0)
    first = jnp.where(core == 0, 0, 1)

    barrier = pltpu.get_barrier_semaphore()
    greeted = (at(1, 0, 0), at(-1, 0, 0), at(0, 1, 0), at(0, -1, 0), at(0, 0, 1), at(0, 0, -1), other)
    for who in greeted:
        pl.semaphore_signal(barrier, inc=1, device_id=who, device_id_type=MESH)

    probe_load = pltpu.make_async_copy(pg_hbm, rawg, lsem.at[0])
    probe_load.start()

    @pl.loop(0, XP)
    def _(c):
        cols = pl.ds(pl.multiple_of(c * LANE, LANE), LANE)
        pltpu.make_async_copy(px_hbm.at[:, cols], slots.at[own, X0 + c], lsem.at[1]).start()

    grad_load = pltpu.make_async_copy(tg_hbm, tg.at[0], lsem.at[2])
    grad_load.start()
    x_load = pltpu.make_async_copy(tx_hbm, tx.at[0], lsem.at[3])
    x_load.start()

    lane = lax.broadcasted_iota(jnp.int32, (1, LANE), 1)
    square[...] = jnp.zeros_like(square)
    square[0:TOP, 0:PROW] = pr_ref[...].astype(F32)
    square[TOP : TOP + 1, 0:PROW] = pe_ref[...].astype(F32)
    square[8 : 8 + TOP, 0:PROW] = pw_ref[...]
    near = square[0:8, :]
    far = pltpu.roll(near, PROW, 1)
    pmarks[...] = jnp.zeros_like(pmarks)
    for g in range(TOP // 2):
        pmarks[g : g + 1, :] = jnp.where(lane < PROW, near[2 * g : 2 * g + 1, :], far[2 * g + 1 : 2 * g + 2, :])
    owner = jnp.where(lane < PROW, near[TOP : TOP + 1, :], far[TOP : TOP + 1, :])
    pmarks[3:4, :] = owner + (z * PEX_ROW).astype(F32)
    slots[own, 0] = pmarks[...].astype(BF)

    turned = jnp.transpose(square[...])
    probe_load.wait()
    for q in range(TOP):
        scale = jnp.broadcast_to(turned[0:PROW, 8 + q : 9 + q], (PROW, LANE))
        for k in range(GP):
            block = rawg[q, :, k * LANE : (k + 1) * LANE].astype(F32)
            slots[own, G0 + k * TOP + q] = (block * scale).astype(BF)
    pltpu.make_async_copy(
        slots.at[own, pl.ds(X0, XP)], slots.at[own, pl.ds(X0, XP)], lsem.at[1]
    ).wait()

    def share(slot, axis, who, begin, count):
        return slots.at[slot, pl.ds(base[axis] + PART * who + begin, count)]

    def zcopies(src, dst):
        out = []
        for axis in range(2):
            out.append(
                pltpu.make_async_remote_copy(
                    src_ref=share(src, axis, rank[axis], 0, PART),
                    dst_ref=share(dst, axis, rank[axis], 0, PART),
                    send_sem=zs.at[dst, axis],
                    recv_sem=zr.at[dst, axis],
                    device_id=znext,
                    device_id_type=MESH,
                )
            )
        out.append(
            pltpu.make_async_remote_copy(
                src_ref=slots.at[src, pl.ds(0, ALONE)],
                dst_ref=slots.at[dst, pl.ds(0, ALONE)],
                send_sem=zs.at[dst, 2],
                recv_sem=zr.at[dst, 2],
                device_id=znext,
                device_id_type=MESH,
            )
        )
        return out

    def ring(slot, axis, kind):
        who = (rank[axis] + (0, 0, NR - 1, 1)[kind]) % NR
        begin, count = ((0, PART), (0, PART), (0, HALF), (HALF, PART - HALF))[kind]
        region = share(slot, axis, who, begin, count)
        return pltpu.make_async_remote_copy(
            src_ref=region,
            dst_ref=region,
            send_sem=rs.at[slot, axis, kind],
            recv_sem=rr.at[slot, axis, kind],
            device_id=sides[axis][kind % 2],
            device_id_type=MESH,
        )

    def landed(slot, axis, kind):
        who = (rank[axis] + (NR - 1, 1, NR - 2, 2)[kind]) % NR
        begin, count = ((0, PART), (0, PART), (0, HALF), (HALF, PART - HALF))[kind]
        region = share(slot, axis, who, begin, count)
        return pltpu.make_async_remote_copy(
            src_ref=region,
            dst_ref=region,
            send_sem=rs.at[slot, axis, kind],
            recv_sem=rr.at[slot, axis, kind],
            device_id=sides[axis][kind % 2],
            device_id_type=MESH,
        )

    pl.semaphore_wait(barrier, len(greeted))
    for copy in zcopies(own, first):
        copy.start()

    marks[0] = jnp.zeros((16, LANE), F32)
    marks[0, 0:TOP, :] = tr_ref[...].astype(F32)
    marks[0, TOP : TOP + 1, :] = te_ref[...].astype(F32)
    square[...] = jnp.zeros_like(square)
    square[0:TOP, :] = tr_ref[...].astype(F32)
    square[8 : 8 + TOP, :] = tw_ref[...]
    turned = jnp.transpose(square[...])
    for r in range(TOP):
        ids[0, r] = jnp.broadcast_to(turned[:, r : r + 1], (TOK, LANE))

    def swap(src, dst, which):
        return pltpu.make_async_remote_copy(
            src_ref=src,
            dst_ref=dst,
            send_sem=es.at[which],
            recv_sem=er.at[which],
            device_id=other,
            device_id_type=MESH,
        )

    swaps = (
        swap(marks.at[0], marks.at[1], 0),
        swap(tx.at[0], tx.at[1], 1),
        swap(tg.at[0], tg.at[1], 2),
    )
    swaps[0].start()
    x_load.wait()
    swaps[1].start()
    grad_load.wait()
    for r in range(TOP):
        scale = jnp.broadcast_to(turned[:, 8 + r : 9 + r], (TOK, LANE))

        @pl.loop(0, GP)
        def _(k):
            cols = pl.ds(pl.multiple_of(k * LANE, LANE), LANE)
            tg[0, r, :, cols] = (tg[0, r, :, cols].astype(F32) * scale).astype(BF)

    swaps[2].start()
    acc[...] = jnp.zeros_like(acc)
    swaps[0].wait_recv()
    square[0:16, :] = marks[1]
    turned = jnp.transpose(square[...])
    for r in range(TOP):
        ids[1, r] = jnp.broadcast_to(turned[:, r : r + 1], (TOK, LANE))
    swaps[1].wait_recv()
    swaps[2].wait_recv()

    def compute(slot):
        px = jnp.concatenate([slots[slot, X0 + c] for c in range(XP)], axis=1)
        px = jnp.concatenate([px, px], axis=0)
        xs[...] = nt(tx[...].reshape(2 * TOK, D), px).reshape(2, TOK, LANE)
        info = slots[slot, 0, 0:16, :].astype(F32)
        rows = lax.broadcasted_iota(jnp.int32, (LANE, LANE), 0).astype(F32)
        probe_marks = (rows == info[3:4, :]).astype(BF)

        @pl.loop(0, 2)
        def _(h):
            pg = jnp.concatenate(
                [
                    slots[slot, G0 + k * TOP : G0 + (k + 1) * TOP].reshape(TOP * PROW, LANE)
                    for k in range(GP)
                ],
                axis=1,
            )
            gram = nt(tg[h].reshape(TOP * TOK, FF), pg)
            total = jnp.zeros((TOK, LANE), F32)
            for r in range(TOP):
                who = ids[h, r]
                for g in range(TOP // 2):
                    part = gram[r * TOK : (r + 1) * TOK, g * LANE : (g + 1) * LANE]
                    total = total + jnp.where(who == info[g : g + 1, :], part, 0.0)
            hi, lo = split(total * xs[h])
            rows16 = lax.broadcasted_iota(jnp.int32, (16, TOK), 0).astype(F32)
            train_marks = (rows16 == marks[h, TOP : TOP + 1, :]).astype(BF)
            sums = jnp.dot(train_marks, hi, preferred_element_type=F32)
            sums = sums + jnp.dot(train_marks, lo, preferred_element_type=F32)
            hi, lo = split(sums)
            acc[h] += nt(hi, probe_marks) + nt(lo, probe_marks)

    def taken(j):
        return (core == 0) | (j >= 1)

    @pl.loop(0, SLOTS + 2)
    def _(j):
        @pl.when((j < SLOTS) & taken(j))
        def _():
            arrived = zcopies(j, j)
            onward = zcopies(j, jnp.minimum(j + 1, SLOTS - 1))
            for part in range(3):
                arrived[part].wait_recv()

                @pl.when(j < SLOTS - 1)
                def _():
                    onward[part].start()

                if part < 2:
                    ring(j, part, 0).start()
                    ring(j, part, 1).start()

        @pl.when((j >= 1) & (j < SLOTS + 1) & taken(j - 1))
        def _():
            slot = jnp.maximum(j - 1, 0)
            for kind in range(2):
                for axis in range(2):
                    landed(slot, axis, kind).wait_recv()
                    ring(slot, axis, kind + 2).start()

        @pl.when(j >= 2)
        def _():
            slot = jnp.maximum(j - 2, 0)

            @pl.when(taken(j - 2))
            def _():
                for kind in range(2, 4):
                    for axis in range(2):
                        landed(slot, axis, kind).wait_recv()

            compute(slot)

    last = swap(acc.at[1], rbuf, 3)
    last.start()
    last.wait_recv()
    out_ref[...] = acc[0, 0:EX_DEV, :] + rbuf[0:EX_DEV, :]

    last.wait_send()
    for copy in swaps:
        copy.wait_send()

    @pl.loop(0, SLOTS)
    def _(j):
        @pl.when(taken(j))
        def _():
            for copy in zcopies(j, j):
                copy.wait_send()
            for axis in range(2):
                for kind in range(4):
                    ring(j, axis, kind).wait_send()


def body(
    train_x,
    train_grad,
    train_routes,
    train_weight,
    train_example,
    probe_x,
    probe_grad,
    probe_routes,
    probe_weight,
    probe_example,
):
    hbm = pl.BlockSpec(memory_space=pl.ANY)
    vmem = pl.BlockSpec(memory_space=pltpu.VMEM)
    dma = pltpu.SemaphoreType.DMA
    return pl.pallas_call(
        kernel,
        out_shape=jax.ShapeDtypeStruct((EX_DEV, LANE), F32),
        in_specs=[hbm, hbm, vmem, vmem, vmem, hbm, hbm, vmem, vmem, vmem],
        out_specs=vmem,
        scratch_shapes=[
            pltpu.VMEM((SLOTS + 1, PANELS, PROW, LANE), BF),
            pltpu.VMEM((2, TOK, D), BF),
            pltpu.VMEM((2, TOP, TOK, FF), BF),
            pltpu.VMEM((TOP, PROW, FF), BF),
            pltpu.VMEM((2, TOP, TOK, LANE), F32),
            pltpu.VMEM((2, 16, LANE), F32),
            pltpu.VMEM((LANE, LANE), F32),
            pltpu.VMEM((PROW, LANE), F32),
            pltpu.VMEM((2, TOK, LANE), F32),
            pltpu.VMEM((2, 16, LANE), F32),
            pltpu.VMEM((16, LANE), F32),
            dma((4,)),
            dma((SLOTS, 3)),
            dma((SLOTS, 3)),
            dma((SLOTS, 2, 4)),
            dma((SLOTS, 2, 4)),
            dma((4,)),
            dma((4,)),
        ],
        compiler_params=pltpu.CompilerParams(
            collective_id=0, has_side_effects=True, vmem_limit_bytes=56 * 1024 * 1024
        ),
        cost_estimate=pl.CostEstimate(flops=16_000_000_000, bytes_accessed=6_000_000, transcendentals=0),
        name="ghost_scores",
    )(
        train_x,
        jnp.transpose(train_grad, (1, 0, 2)),
        train_routes.T,
        train_weight.T,
        train_example[None, :],
        probe_x,
        jnp.transpose(probe_grad, (1, 0, 2)),
        probe_routes.T,
        probe_weight.T,
        probe_example[None, :],
    )


def solution(mesh):
    in_specs = (
        P(("dp", "expert"), None),
        P(("dp", "expert"), None, None),
        P(("dp", "expert"), None),
        P(("dp", "expert"), None),
        P(("dp", "expert")),
        P("dp", None),
        P("dp", None, None),
        P("dp", None),
        P("dp", None),
        P("dp"),
    )
    out_specs = P(("dp", "expert"), None)
    return jax.shard_map(body, mesh=mesh, in_specs=in_specs, out_specs=out_specs, check_vma=False)
```

time: 289 us -> 88.8 us (0.31)
  blocking collectives: 92.3 us -> 0 us
  Pallas kernels: 0 us -> 87.3 us
  local copies, waits for them, and re-layouts: 78.2 us -> 1.26 us
  waiting for transfers between devices: 50.6 us -> 0 us
  other arithmetic: 19.4 us -> 0 us
  starting transfers between devices: 18.8 us -> 0 us
  matrix products: 14.7 us -> 0 us
  between operations: 13.8 us -> 0.01 us
    pallas_call x0 -> x1, Pallas kernels: none -> 87.3 us  [body(): pl.pallas_call(kernel, out_shape=jax.ShapeDtypeStruct((EX_DEV, LANE), F32...]
    all_gather x2 -> x0, blocking collectives: 70.1 us -> none  [the longest x1 40.9 us: body(): lax.all_gather(probe_gsel, 'dp', axis=1, tiled=True)]
    all_to_all x2 -> x0, waiting for transfers between devices: 50.6 us -> none  [the longest x1 40.6 us: body(): lax.all_to_all(feature_slots, 'expert', split_axis=0, concat_axis=0, tile...]
    gather x10 -> x0, local copies, waits for them, and re-layouts: 41.2 us -> none  [the longest x2 19.3 us: body(): train_x[home_token]]
    all_to_all x1 -> x0, blocking collectives: 22.2 us -> none  [body(): lax.all_to_all(per_probe, 'expert', split_axis=0, concat_axis=0, tiled=True)]
    all_to_all x2 -> x0, starting transfers between devices: 18.7 us -> none  [the longest x1 11.3 us: body(): lax.all_to_all(grad_slots, 'expert', split_axis=0, concat_axis=0, tiled=T...]
    all_to_all x2 -> x0, local copies, waits for them, and re-layouts: 18.3 us -> none  [the longest x1 13.1 us: body(): lax.all_to_all(feature_slots, 'expert', split_axis=0, concat_axis=0, tile...]
    select_n x7 -> x0, other arithmetic: 14.8 us -> none  [the longest x1 10 us: body(): jnp.where(home_valid[:, None], train_x[home_token], 0)]
  transfers between devices with their start and end apart: 3 -> 0, of which waited for: 2 -> 0; matrix products, arithmetic and copies ran while one was open for 20% -> 0% of each run, Pallas kernels for 0% -> 0%
where the time goes in v1:
time: 88.8 us; the launch traced here: 88.6 us
  Pallas kernels  87.3 us (98%)
  local copies, waits for them, and re-layouts  1.26 us (1%)
    pallas_call x1, Pallas kernels, body(): pl.pallas_call(kernel, out_shape=jax.ShapeDtypeStruct((EX_DEV, LANE), F32...  87.3 us

profile of v1, /device:TPU:1, one launch (start us, length us, event | category | flops | bytes accessed | tf_op | source)
XLA Modules:
  0.0 88.6 jit_solution(7158053488695270576)
XLA Ops:
  0.0 87.3 %ghost_scores.1 = f32[4,128]{1,0:T(4,128)} custom-call(bf16[128,5120]{1,0:T(8,128)(2,1)} %tx_hbm.1, bf16[6,128,1536]{2,1,0:T(8,128)(2,1)} %bitcast.8, s32[6,128]{1,0:T(8,128)} %bitcast.10, f32[6,128]{1,0:T(8,128)} %bitcast.11, s32[1,128]{1,0:T(1,128)} %bitcast.14, bf16[64,5120]{1,0:T(8,128)(2,1)} %px_hbm.1, bf16[6,64,1536]{2,1,0:T(8,128)(2,1)} %bitcast.9, ...), custom_call_target="tpu_custom_call" | custom-call | flops 16000000000 | bytes 6000000 | tf_op jit(solution)/shard_map/ghost_scores/pallas_call | solution.py:351
  87.3 1.3 %copy.12 = f32[4,128]{1,0:T(4,128)} copy(f32[4,128]{1,0:T(4,128)} %ghost_scores.1) | data formatting | bytes 4096

commit v2 on v1

--- a/solution.py
+++ b/solution.py
@@ -30,6 +30,7 @@
 ALONE = 1 + 8
 PART = (PANELS - ALONE) // (2 * NR)
 HALF = (PART + 1) // 2
+LAG = 3
 
 
 def nt(a, b):
@@ -233,65 +234,72 @@
 
     swaps[2].start()
     acc[...] = jnp.zeros_like(acc)
-    swaps[0].wait_recv()
-    square[0:16, :] = marks[1]
-    turned = jnp.transpose(square[...])
-    for r in range(TOP):
-        ids[1, r] = jnp.broadcast_to(turned[:, r : r + 1], (TOK, LANE))
-    swaps[1].wait_recv()
-    swaps[2].wait_recv()
-
-    def compute(slot):
+
+    def meet():
+        swaps[0].wait_recv()
+        square[0:16, :] = marks[1]
+        turned = jnp.transpose(square[...])
+        for r in range(TOP):
+            ids[1, r] = jnp.broadcast_to(turned[:, r : r + 1], (TOK, LANE))
+        swaps[1].wait_recv()
+        swaps[2].wait_recv()
+
+    def feature_gram(slot):
         px = jnp.concatenate([slots[slot, X0 + c] for c in range(XP)], axis=1)
         px = jnp.concatenate([px, px], axis=0)
         xs[...] = nt(tx[...].reshape(2 * TOK, D), px).reshape(2, TOK, LANE)
+
+    def route_gram(slot, h):
         info = slots[slot, 0, 0:16, :].astype(F32)
         rows = lax.broadcasted_iota(jnp.int32, (LANE, LANE), 0).astype(F32)
         probe_marks = (rows == info[3:4, :]).astype(BF)
-
-        @pl.loop(0, 2)
-        def _(h):
-            pg = jnp.concatenate(
-                [
-                    slots[slot, G0 + k * TOP : G0 + (k + 1) * TOP].reshape(TOP * PROW, LANE)
-                    for k in range(GP)
-                ],
-                axis=1,
-            )
-            gram = nt(tg[h].reshape(TOP * TOK, FF), pg)
-            total = jnp.zeros((TOK, LANE), F32)
-            for r in range(TOP):
-                who = ids[h, r]
-                for g in range(TOP // 2):
-                    part = gram[r * TOK : (r + 1) * TOK, g * LANE : (g + 1) * LANE]
-                    total = total + jnp.where(who == info[g : g + 1, :], part, 0.0)
-            hi, lo = split(total * xs[h])
-            rows16 = lax.broadcasted_iota(jnp.int32, (16, TOK), 0).astype(F32)
-            train_marks = (rows16 == marks[h, TOP : TOP + 1, :]).astype(BF)
-            sums = jnp.dot(train_marks, hi, preferred_element_type=F32)
-            sums = sums + jnp.dot(train_marks, lo, preferred_element_type=F32)
-            hi, lo = split(sums)
-            acc[h] += nt(hi, probe_marks) + nt(lo, probe_marks)
+        pg = jnp.concatenate(
+            [slots[slot, G0 + k * TOP : G0 + (k + 1) * TOP].reshape(TOP * PROW, LANE) for k in range(GP)],
+            axis=1,
+        )
+        gram = nt(tg[h].reshape(TOP * TOK, FF), pg)
+        total = jnp.zeros((TOK, LANE), F32)
+        for r in range(TOP):
+            who = ids[h, r]
+            for g in range(TOP // 2):
+                part = gram[r * TOK : (r + 1) * TOK, g * LANE : (g + 1) * LANE]
+                total = total + jnp.where(who == info[g : g + 1, :], part, 0.0)
+        hi, lo = split(total * xs[h])
+        rows16 = lax.broadcasted_iota(jnp.int32, (16, TOK), 0).astype(F32)
+        train_marks = (rows16 == marks[h, TOP : TOP + 1, :]).astype(BF)
+        sums = jnp.dot(train_marks, hi, preferred_element_type=F32)
+        sums = sums + jnp.dot(train_marks, lo, preferred_element_type=F32)
+        hi, lo = split(sums)
+        acc[h] += nt(hi, probe_marks) + nt(lo, probe_marks)
 
     def taken(j):
         return (core == 0) | (j >= 1)
 
-    @pl.loop(0, SLOTS + 2)
+    @pl.loop(0, SLOTS + LAG)
     def _(j):
-        @pl.when((j < SLOTS) & taken(j))
-        def _():
-            arrived = zcopies(j, j)
-            onward = zcopies(j, jnp.minimum(j + 1, SLOTS - 1))
-            for part in range(3):
-                arrived[part].wait_recv()
+        fresh = (j < SLOTS) & taken(j)
+        ready = j >= LAG
+        done = jnp.maximum(j - LAG, 0)
+
+        def pass_on(part):
+            @pl.when(fresh)
+            def _():
+                zcopies(j, j)[part].wait_recv()
 
                 @pl.when(j < SLOTS - 1)
                 def _():
-                    onward[part].start()
+                    zcopies(j, jnp.minimum(j + 1, SLOTS - 1))[part].start()
 
                 if part < 2:
                     ring(j, part, 0).start()
                     ring(j, part, 1).start()
+
+        pass_on(0)
+        pl.when(ready)(lambda: feature_gram(done))
+        pass_on(1)
+        pl.when(ready)(lambda: route_gram(done, 0))
+        pass_on(2)
+        pl.when(j == LAG - 1)(meet)
 
         @pl.when((j >= 1) & (j < SLOTS + 1) & taken(j - 1))
         def _():
@@ -301,17 +309,14 @@
                     landed(slot, axis, kind).wait_recv()
                     ring(slot, axis, kind + 2).start()
 
-        @pl.when(j >= 2)
+        pl.when(ready)(lambda: route_gram(done, 1))
+
+        @pl.when((j >= 2) & (j < SLOTS + 2) & taken(j - 2))
         def _():
             slot = jnp.maximum(j - 2, 0)
-
-            @pl.when(taken(j - 2))
-            def _():
-                for kind in range(2, 4):
-                    for axis in range(2):
-                        landed(slot, axis, kind).wait_recv()
-
-            compute(slot)
+            for kind in range(2, 4):
+                for axis in range(2):
+                    landed(slot, axis, kind).wait_recv()
 
     last = swap(acc.at[1], rbuf, 3)
     last.start()

time: 88.8 us -> 85.6 us (0.964)
  Pallas kernels: 87.3 us -> 84.1 us
    pallas_call x1, Pallas kernels: 87.3 us -> 84.1 us  [body(): pl.pallas_call(kernel, out_shape=jax.ShapeDtypeStruct((EX_DEV, LANE), F32...]
where the time goes in v2:
time: 85.6 us; the launch traced here: 85.4 us
  Pallas kernels  84.1 us (98%)
  local copies, waits for them, and re-layouts  1.26 us (1%)
    pallas_call x1, Pallas kernels, body(): pl.pallas_call(kernel, out_shape=jax.ShapeDtypeStruct((EX_DEV, LANE), F32...  84.1 us

profile of v2, /device:TPU:1, one launch (start us, length us, event | category | flops | bytes accessed | tf_op | source)
XLA Modules:
  0.0 85.4 jit_solution(1254052919904710932)
XLA Ops:
  0.0 84.1 %ghost_scores.1 = f32[4,128]{1,0:T(4,128)} custom-call(bf16[128,5120]{1,0:T(8,128)(2,1)} %tx_hbm.1, bf16[6,128,1536]{2,1,0:T(8,128)(2,1)} %bitcast.8, s32[6,128]{1,0:T(8,128)} %bitcast.10, f32[6,128]{1,0:T(8,128)} %bitcast.11, s32[1,128]{1,0:T(1,128)} %bitcast.14, bf16[64,5120]{1,0:T(8,128)(2,1)} %px_hbm.1, bf16[6,64,1536]{2,1,0:T(8,128)(2,1)} %bitcast.9, ...), custom_call_target="tpu_custom_call" | custom-call | flops 16000000000 | bytes 6000000 | tf_op jit(solution)/shard_map/ghost_scores/pallas_call | solution.py:356
  84.2 1.3 %copy.12 = f32[4,128]{1,0:T(4,128)} copy(f32[4,128]{1,0:T(4,128)} %ghost_scores.1) | data formatting | bytes 4096

commit v3 on v2

v3 whole, which is shorter than its diff:
```python
import jax
import jax.numpy as jnp
from jax import lax
from jax.experimental import pallas as pl
from jax.experimental.pallas import tpu as pltpu
from jax.sharding import PartitionSpec as P

MESH = pl.DeviceIdType.MESH
BF = jnp.bfloat16
F32 = jnp.float32

LANE = 128
TOK = 128
PROW = 64
TOP = 6
D = 5120
FF = 1536
NZ = 16
NR = 4
SLOTS = 8
OWN = SLOTS
PEX_ROW = 8
EX_DEV = 4

KH = FF // 2

XP = D // LANE
GP = KH // LANE
X0 = 1
G0 = X0 + XP
PANELS = G0 + GP * TOP
YPART = 11
XPART = 5
YBASE = PANELS - NR * YPART
XBASE = YBASE - NR * XPART
HALF = (YPART + 1) // 2
LAG = 3
PAIR = 6


def nt(a, b):
    return lax.dot_general(a, b, (((1,), (1,)), ((), ())), preferred_element_type=F32)


def split(v):
    hi = v.astype(BF)
    return hi, (v - hi.astype(F32)).astype(BF)


def kernel(
    tx_hbm,
    tg_hbm,
    tr_ref,
    tw_ref,
    te_ref,
    px_hbm,
    pg_hbm,
    pr_ref,
    pw_ref,
    pe_ref,
    out_ref,
    slots,
    tx,
    tg,
    away,
    rawg,
    ids,
    marks,
    square,
    pmarks,
    xs,
    near_sum,
    far_sum,
    back_sum,
    acc,
    rbuf,
    lsem,
    zs,
    zr,
    rs,
    rr,
    es,
    er,
    qs,
    qr,
):
    z = lax.axis_index("dp")
    e = lax.axis_index("expert")
    core = e % 2
    xi = (e // 2) % NR
    yi = e // (2 * NR)
    odd = xi % 2

    def at(zz, xx, yy, cc):
        return (zz, (yy * NR + xx) * 2 + cc)

    xp = xi + 1 - 2 * odd
    xn = (xi + NR - 1 + 2 * odd) % NR
    other = at(z, xi, yi, 1 - core)
    partner = at(z, xp, yi, core)
    across = at(z, xp, yi, 1 - core)
    beside = at(z, xn, yi, core)
    right = at(z, xi, (yi + 1) % NR, core)
    left = at(z, xi, (yi + NR - 1) % NR, core)
    above = at((z + 1) % NZ, xi, yi, core)
    below = at((z + NZ - 1) % NZ, xi, yi, core)
    znext = at((z + NZ - 1 + 2 * core) % NZ, xi, yi, core)
    own = jnp.where(core == 0, OWN, 0)
    first = jnp.where(core == 0, 0, 1)

    barrier = pltpu.get_barrier_semaphore()
    greeted = (other, partner, across, beside, right, left, above, below)
    for who in greeted:
        pl.semaphore_signal(barrier, inc=1, device_id=who, device_id_type=MESH)

    mine = pl.ds(pl.multiple_of(odd * KH, LANE), KH)
    theirs = pl.ds(pl.multiple_of((1 - odd) * KH, LANE), KH)
    probe_load = pltpu.make_async_copy(pg_hbm.at[:, :, mine], rawg, lsem.at[0])
    probe_load.start()

    @pl.loop(0, XP)
    def _(c):
        cols = pl.ds(pl.multiple_of(c * LANE, LANE), LANE)
        pltpu.make_async_copy(px_hbm.at[:, cols], slots.at[own, X0 + c], lsem.at[1]).start()

    away_load = pltpu.make_async_copy(tg_hbm.at[:, :, theirs], away, lsem.at[4])
    away_load.start()
    grad_load = pltpu.make_async_copy(tg_hbm.at[:, :, mine], tg.at[0], lsem.at[2])
    grad_load.start()
    x_load = pltpu.make_async_copy(tx_hbm, tx.at[0], lsem.at[3])
    x_load.start()

    lane = lax.broadcasted_iota(jnp.int32, (1, LANE), 1)
    square[...] = jnp.zeros_like(square)
    square[0:TOP, 0:PROW] = pr_ref[...].astype(F32)
    square[TOP : TOP + 1, 0:PROW] = pe_ref[...].astype(F32)
    square[8 : 8 + TOP, 0:PROW] = pw_ref[...]
    near = square[0:8, :]
    far = pltpu.roll(near, PROW, 1)
    pmarks[...] = jnp.zeros_like(pmarks)
    for g in range(TOP // 2):
        pmarks[g : g + 1, :] = jnp.where(lane < PROW, near[2 * g : 2 * g + 1, :], far[2 * g + 1 : 2 * g + 2, :])
    owner = jnp.where(lane < PROW, near[TOP : TOP + 1, :], far[TOP : TOP + 1, :])
    pmarks[3:4, :] = owner + (z * PEX_ROW).astype(F32)
    slots[own, 0] = pmarks[...].astype(BF)

    turned = jnp.transpose(square[...])
    probe_load.wait()
    for q in range(TOP):
        scale = jnp.broadcast_to(turned[0:PROW, 8 + q : 9 + q], (PROW, LANE))
        for k in range(GP):
            block = rawg[q, :, k * LANE : (k + 1) * LANE].astype(F32)
            slots[own, G0 + k * TOP + q] = (block * scale).astype(BF)
    pltpu.make_async_copy(slots.at[own, pl.ds(X0, XP)], slots.at[own, pl.ds(X0, XP)], lsem.at[1]).wait()

    def remote(src, dst, send, recv, who):
        return pltpu.make_async_remote_copy(
            src_ref=src, dst_ref=dst, send_sem=send, recv_sem=recv, device_id=who, device_id_type=MESH
        )

    def yshare(slot, who, begin, count):
        return slots.at[slot, pl.ds(YBASE + YPART * who + begin, count)]

    def xshare(slot, who):
        return slots.at[slot, pl.ds(XBASE + XPART * who, XPART)]

    def zcopy(src, dst, part):
        if part == 0:
            pick = lambda slot: yshare(slot, yi, 0, YPART)
        elif part == 1:
            pick = lambda slot: xshare(slot, xi)
        else:
            pick = lambda slot: slots.at[slot, pl.ds(0, XBASE)]
        return remote(pick(src), pick(dst), zs.at[dst, part], zr.at[dst, part], znext)

    def yring(slot, kind, landing=False):
        who = (0, 0, NR - 1, 1)[kind] + ((NR - 1, 1)[kind % 2] if landing else 0)
        begin, count = ((0, YPART), (0, YPART), (0, HALF), (HALF, YPART - HALF))[kind]
        region = yshare(slot, (yi + who) % NR, begin, count)
        return remote(region, region, rs.at[slot, 0, kind], rr.at[slot, 0, kind], (right, left)[kind % 2])

    def xring(slot, kind, landing=False):
        who = (xp, xn, (xi + 2) % NR)[kind] if landing else (xi, xi, xp)[kind]
        region = xshare(slot, who)
        return remote(region, region, rs.at[slot, 1, kind], rr.at[slot, 1, kind], (partner, beside, beside)[kind])

    pl.semaphore_wait(barrier, len(greeted))
    for part in range(3):
        zcopy(own, first, part).start()

    marks[0] = jnp.zeros((16, LANE), F32)
    marks[0, 0:TOP, :] = tr_ref[...].astype(F32)
    marks[0, TOP : TOP + 1, :] = te_ref[...].astype(F32)
    square[...] = jnp.zeros_like(square)
    square[0:TOP, :] = tr_ref[...].astype(F32)
    square[8 : 8 + TOP, :] = tw_ref[...]
    turned = jnp.transpose(square[...])

    def scale_train(ref):
        for r in range(TOP):
            scale = jnp.broadcast_to(turned[:, 8 + r : 9 + r], (TOK, LANE))

            @pl.loop(0, GP)
            def _(k):
                cols = pl.ds(pl.multiple_of(k * LANE, LANE), LANE)
                ref[r, :, cols] = (ref[r, :, cols].astype(F32) * scale).astype(BF)

    def spread(group):
        square[0:16, :] = marks[group]
        columns = jnp.transpose(square[...])
        for r in range(TOP):
            ids[group, r] = jnp.broadcast_to(columns[:, r : r + 1], (TOK, LANE))

    def swap(src, dst, which, who):
        return remote(src, dst, es.at[which], er.at[which], who)

    swaps = (
        swap(marks.at[0], marks.at[1], 0, other),
        swap(marks.at[0], marks.at[2], 1, partner),
        swap(marks.at[0], marks.at[3], 2, across),
        swap(away, tg.at[2], 3, partner),
        swap(tx.at[0], tx.at[1], 4, other),
        swap(tg.at[0], tg.at[1], 5, other),
        swap(tg.at[2], tg.at[3], 6, other),
    )
    away_load.wait()
    scale_train(away)
    swaps[3].start()
    for which in range(3):
        swaps[which].start()
    x_load.wait()
    swaps[4].start()
    grad_load.wait()
    scale_train(tg.at[0])
    swaps[5].start()
    spread(0)

    def meet_core():
        swaps[0].wait_recv()
        spread(1)
        swaps[4].wait_recv()
        swaps[5].wait_recv()

    def meet_partner():
        swaps[3].wait_recv()
        swaps[6].start()
        for group in (2, 3):
            swaps[group - 1].wait_recv()
            spread(group)

    def feature_gram(slot):
        px = jnp.concatenate([slots[slot, X0 + c] for c in range(XP)], axis=1)
        px = jnp.concatenate([px, px], axis=0)
        gram = nt(tx[...].reshape(2 * TOK, D), px)
        xs[slot] = jnp.where(lane < PROW, gram[0:TOK, :], gram[TOK : 2 * TOK, :])

    def route_gram(slot, chip):
        info = slots[slot, 0, 0:16, :].astype(F32)
        pg = jnp.concatenate(
            [slots[slot, G0 + k * TOP : G0 + (k + 1) * TOP].reshape(TOP * PROW, LANE) for k in range(GP)],
            axis=1,
        )
        gram = nt(tg[2 * chip : 2 * chip + 2].reshape(2 * TOP * TOK, KH), pg)
        sums = []
        for h in range(2):
            total = jnp.zeros((TOK, LANE), F32)
            for r in range(TOP):
                who = ids[2 * chip + h, r]
                row = (h * TOP + r) * TOK
                for g in range(TOP // 2):
                    part = gram[row : row + TOK, g * LANE : (g + 1) * LANE]
                    total = total + jnp.where(who == info[g : g + 1, :], part, 0.0)
            sums.append(total + pltpu.roll(total, PROW, 1))
        return jnp.where(lane < PROW, sums[0], sums[1])

    def give_back(slot):
        return remote(far_sum.at[slot], back_sum.at[slot], qs.at[slot], qr.at[slot], partner)

    def own_tokens(slot):
        near_sum[slot] = route_gram(slot, 0)

    def taken(j):
        return (core == 0) | (j >= 1)

    @pl.loop(0, SLOTS + LAG)
    def _(j):
        fresh = (j < SLOTS) & taken(j)
        ready = j >= LAG
        done = jnp.maximum(j - LAG, 0)

        def pass_on(part):
            @pl.when(fresh)
            def _():
                zcopy(j, j, part).wait_recv()

                @pl.when(j < SLOTS - 1)
                def _():
                    zcopy(j, jnp.minimum(j + 1, SLOTS - 1), part).start()

                if part == 0:
                    yring(j, 0).start()
                    yring(j, 1).start()
                if part == 1:
                    xring(j, 0).start()
                    xring(j, 1).start()

        pass_on(0)
        pl.when(ready)(lambda: feature_gram(done))
        pass_on(1)

        @pl.when(j >= PAIR)
        def _():
            @pl.when(j == PAIR)
            def _():
                swaps[6].wait_recv()

            late = 2 * (j - PAIR)
            begin = jnp.where(late < j - LAG, late, j - LAG)
            end = jnp.where(late < j - LAG, late + 2, j - LAG + 1)

            @pl.loop(begin, end)
            def _(slot):
                far_sum[slot] = route_gram(slot, 1).astype(BF)
                give_back(slot).start()

        pass_on(2)
        pl.when(j == LAG - 1)(meet_core)
        pl.when(j == PAIR - 1)(meet_partner)

        @pl.when((j >= 1) & (j < SLOTS + 1) & taken(j - 1))
        def _():
            slot = jnp.maximum(j - 1, 0)
            for kind in range(2):
                yring(slot, kind, True).wait_recv()
                yring(slot, kind + 2).start()
                if kind == 0:
                    xring(slot, 0, True).wait_recv()
                    xring(slot, 2).start()

        pl.when(ready)(lambda: own_tokens(done))

        @pl.when((j >= 2) & (j < SLOTS + 2) & taken(j - 2))
        def _():
            slot = jnp.maximum(j - 2, 0)
            for kind in range(2, 4):
                yring(slot, kind, True).wait_recv()
            for kind in range(1, 3):
                xring(slot, kind, True).wait_recv()

    values, owners = [], []
    rows = lax.broadcasted_iota(jnp.int32, (LANE, LANE), 0).astype(F32)
    for slot in range(SLOTS):
        give_back(slot).wait_recv()
        values.append((near_sum[slot] + back_sum[slot].astype(F32)) * xs[slot])
        owners.append((rows == slots[slot, 0, 0:16, :].astype(F32)[3:4, :]).astype(BF))
    hi, lo = split(jnp.concatenate(values, axis=1))
    owners = jnp.concatenate(owners, axis=1)
    eights = lax.broadcasted_iota(jnp.int32, (8, TOK), 0).astype(F32)
    examples = [(eights == marks[h, TOP : TOP + 1, :]).astype(F32) for h in range(2)]
    examples = jnp.concatenate(examples, axis=0).astype(BF)
    sums = jnp.dot(examples, hi, preferred_element_type=F32) + jnp.dot(examples, lo, preferred_element_type=F32)
    shape = (16, SLOTS * LANE)
    first_core = lax.broadcasted_iota(jnp.int32, shape, 0) < 8
    first_half = lax.broadcasted_iota(jnp.int32, shape, 1) % LANE < PROW
    hi, lo = split(jnp.where(first_core == first_half, sums, 0.0))
    acc[...] = nt(hi, owners) + nt(lo, owners)

    last = swap(acc.at[pl.ds(8, 8)], rbuf, 7, other)
    last.start()
    last.wait_recv()
    out_ref[...] = acc[0:EX_DEV, :] + rbuf[0:EX_DEV, :]

    last.wait_send()
    for copy in swaps:
        copy.wait_send()

    @pl.loop(0, SLOTS)
    def _(j):
        give_back(j).wait_send()

        @pl.when(taken(j))
        def _():
            for part in range(3):
                zcopy(j, j, part).wait_send()
            for kind in range(4):
                yring(j, kind).wait_send()
            for kind in range(3):
                xring(j, kind).wait_send()


def body(
    train_x,
    train_grad,
    train_routes,
    train_weight,
    train_example,
    probe_x,
    probe_grad,
    probe_routes,
    probe_weight,
    probe_example,
):
    hbm = pl.BlockSpec(memory_space=pl.ANY)
    vmem = pl.BlockSpec(memory_space=pltpu.VMEM)
    dma = pltpu.SemaphoreType.DMA
    return pl.pallas_call(
        kernel,
        out_shape=jax.ShapeDtypeStruct((EX_DEV, LANE), F32),
        in_specs=[hbm, hbm, vmem, vmem, vmem, hbm, hbm, vmem, vmem, vmem],
        out_specs=vmem,
        scratch_shapes=[
            pltpu.VMEM((SLOTS + 1, PANELS, PROW, LANE), BF),
            pltpu.VMEM((2, TOK, D), BF),
            pltpu.VMEM((4, TOP, TOK, KH), BF),
            pltpu.VMEM((TOP, TOK, KH), BF),
            pltpu.VMEM((TOP, PROW, KH), BF),
            pltpu.VMEM((4, TOP, TOK, LANE), F32),
            pltpu.VMEM((4, 16, LANE), F32),
            pltpu.VMEM((LANE, LANE), F32),
            pltpu.VMEM((PROW, LANE), F32),
            pltpu.VMEM((SLOTS, TOK, LANE), F32),
            pltpu.VMEM((SLOTS, TOK, LANE), F32),
            pltpu.VMEM((SLOTS, TOK, LANE), BF),
            pltpu.VMEM((SLOTS, TOK, LANE), BF),
            pltpu.VMEM((16, LANE), F32),
            pltpu.VMEM((8, LANE), F32),
            dma((5,)),
            dma((SLOTS, 3)),
            dma((SLOTS, 3)),
            dma((SLOTS, 2, 4)),
            dma((SLOTS, 2, 4)),
            dma((8,)),
            dma((8,)),
            dma((SLOTS,)),
            dma((SLOTS,)),
        ],
        compiler_params=pltpu.CompilerParams(
            collective_id=0, has_side_effects=True, vmem_limit_bytes=56 * 1024 * 1024
        ),
        cost_estimate=pl.CostEstimate(flops=16_000_000_000, bytes_accessed=6_000_000, transcendentals=0),
        name="ghost_scores",
    )(
        train_x,
        jnp.transpose(train_grad, (1, 0, 2)),
        train_routes.T,
        train_weight.T,
        train_example[None, :],
        probe_x,
        jnp.transpose(probe_grad, (1, 0, 2)),
        probe_routes.T,
        probe_weight.T,
        probe_example[None, :],
    )


def solution(mesh):
    in_specs = (
        P(("dp", "expert"), None),
        P(("dp", "expert"), None, None),
        P(("dp", "expert"), None),
        P(("dp", "expert"), None),
        P(("dp", "expert")),
        P("dp", None),
        P("dp", None, None),
        P("dp", None),
        P("dp", None),
        P("dp"),
    )
    out_specs = P(("dp", "expert"), None)
    return jax.shard_map(body, mesh=mesh, in_specs=in_specs, out_specs=out_specs, check_vma=False)
```

time: 85.6 us -> 94.6 us (1.11)
  Pallas kernels: 84.1 us -> 93.2 us
    pallas_call x1, Pallas kernels: 84.1 us -> 93.2 us  [body(): pl.pallas_call(kernel, out_shape=jax.ShapeDtypeStruct((EX_DEV, LANE), F32...]
where the time goes in v3:
time: 94.6 us; the launch traced here: 94.5 us
  Pallas kernels  93.2 us (99%)
  local copies, waits for them, and re-layouts  1.26 us (1%)
    pallas_call x1, Pallas kernels, body(): pl.pallas_call(kernel, out_shape=jax.ShapeDtypeStruct((EX_DEV, LANE), F32...  93.2 us

profile of v3, /device:TPU:1, one launch (start us, length us, event | category | flops | bytes accessed | tf_op | source)
XLA Modules:
  0.0 94.5 jit_solution(3477732704953404007)
XLA Ops:
  0.0 93.2 %ghost_scores.1 = f32[4,128]{1,0:T(4,128)} custom-call(bf16[128,5120]{1,0:T(8,128)(2,1)} %tx_hbm.1, bf16[6,128,1536]{2,1,0:T(8,128)(2,1)} %bitcast.8, s32[6,128]{1,0:T(8,128)} %bitcast.10, f32[6,128]{1,0:T(8,128)} %bitcast.11, s32[1,128]{1,0:T(1,128)} %bitcast.14, bf16[64,5120]{1,0:T(8,128)(2,1)} %px_hbm.1, bf16[6,64,1536]{2,1,0:T(8,128)(2,1)} %bitcast.9, ...), custom_call_target="tpu_custom_call" | custom-call | flops 16000000000 | bytes 6000000 | tf_op jit(solution)/shard_map/ghost_scores/pallas_call | solution.py:406
  93.2 1.3 %copy.12 = f32[4,128]{1,0:T(4,128)} copy(f32[4,128]{1,0:T(4,128)} %ghost_scores.1) | data formatting | bytes 4096

commit v4 on v2

--- a/solution.py
+++ b/solution.py
@@ -30,7 +30,7 @@
 ALONE = 1 + 8
 PART = (PANELS - ALONE) // (2 * NR)
 HALF = (PART + 1) // 2
-LAG = 3
+LAG = 4
 
 
 def nt(a, b):
@@ -118,12 +118,10 @@
     square[TOP : TOP + 1, 0:PROW] = pe_ref[...].astype(F32)
     square[8 : 8 + TOP, 0:PROW] = pw_ref[...]
     near = square[0:8, :]
-    far = pltpu.roll(near, PROW, 1)
+    both = near + pltpu.roll(near, PROW, 1)
     pmarks[...] = jnp.zeros_like(pmarks)
-    for g in range(TOP // 2):
-        pmarks[g : g + 1, :] = jnp.where(lane < PROW, near[2 * g : 2 * g + 1, :], far[2 * g + 1 : 2 * g + 2, :])
-    owner = jnp.where(lane < PROW, near[TOP : TOP + 1, :], far[TOP : TOP + 1, :])
-    pmarks[3:4, :] = owner + (z * PEX_ROW).astype(F32)
+    pmarks[0:TOP, :] = both[0:TOP, :]
+    pmarks[TOP : TOP + 1, :] = both[TOP : TOP + 1, :] + (z * PEX_ROW).astype(F32)
     slots[own, 0] = pmarks[...].astype(BF)
 
     turned = jnp.transpose(square[...])
@@ -244,26 +242,33 @@
         swaps[1].wait_recv()
         swaps[2].wait_recv()
 
-    def feature_gram(slot):
-        px = jnp.concatenate([slots[slot, X0 + c] for c in range(XP)], axis=1)
-        px = jnp.concatenate([px, px], axis=0)
+    def feature_gram(pair):
+        px = jnp.concatenate(
+            [jnp.concatenate([slots[2 * pair + i, X0 + c] for c in range(XP)], axis=1) for i in range(2)], axis=0
+        )
         xs[...] = nt(tx[...].reshape(2 * TOK, D), px).reshape(2, TOK, LANE)
 
-    def route_gram(slot, h):
-        info = slots[slot, 0, 0:16, :].astype(F32)
+    def route_gram(pair, h):
+        info = [slots[2 * pair + i, 0, 0:16, :].astype(F32) for i in range(2)]
+        info = jnp.where(lane < PROW, info[0], info[1])
         rows = lax.broadcasted_iota(jnp.int32, (LANE, LANE), 0).astype(F32)
-        probe_marks = (rows == info[3:4, :]).astype(BF)
+        probe_marks = (rows == info[TOP : TOP + 1, :]).astype(BF)
         pg = jnp.concatenate(
-            [slots[slot, G0 + k * TOP : G0 + (k + 1) * TOP].reshape(TOP * PROW, LANE) for k in range(GP)],
+            [
+                jnp.concatenate(
+                    [slots[2 * pair + i, G0 + k * TOP + q] for q in range(TOP) for i in range(2)], axis=0
+                )
+                for k in range(GP)
+            ],
             axis=1,
         )
         gram = nt(tg[h].reshape(TOP * TOK, FF), pg)
         total = jnp.zeros((TOK, LANE), F32)
         for r in range(TOP):
             who = ids[h, r]
-            for g in range(TOP // 2):
-                part = gram[r * TOK : (r + 1) * TOK, g * LANE : (g + 1) * LANE]
-                total = total + jnp.where(who == info[g : g + 1, :], part, 0.0)
+            for q in range(TOP):
+                part = gram[r * TOK : (r + 1) * TOK, q * LANE : (q + 1) * LANE]
+                total = total + jnp.where(who == info[q : q + 1, :], part, 0.0)
         hi, lo = split(total * xs[h])
         rows16 = lax.broadcasted_iota(jnp.int32, (16, TOK), 0).astype(F32)
         train_marks = (rows16 == marks[h, TOP : TOP + 1, :]).astype(BF)
@@ -279,7 +284,8 @@
     def _(j):
         fresh = (j < SLOTS) & taken(j)
         ready = j >= LAG
-        done = jnp.maximum(j - LAG, 0)
+        since = jnp.maximum(j - LAG, 0)
+        pair, half = since // 2, since % 2
 
         def pass_on(part):
             @pl.when(fresh)
@@ -295,9 +301,9 @@
                     ring(j, part, 1).start()
 
         pass_on(0)
-        pl.when(ready)(lambda: feature_gram(done))
+        pl.when(ready & (half == 0))(lambda: feature_gram(pair))
         pass_on(1)
-        pl.when(ready)(lambda: route_gram(done, 0))
+        pl.when(ready)(lambda: route_gram(pair, half))
         pass_on(2)
         pl.when(j == LAG - 1)(meet)
 
@@ -308,8 +314,6 @@
                 for axis in range(2):
                     landed(slot, axis, kind).wait_recv()
                     ring(slot, axis, kind + 2).start()
-
-        pl.when(ready)(lambda: route_gram(done, 1))
 
         @pl.when((j >= 2) & (j < SLOTS + 2) & taken(j - 2))
         def _():

time: 85.6 us -> 85.7 us (level)
  no operation moved by 1% of the time
where the time goes in v4:
time: 85.7 us; the launch traced here: 85.6 us
  Pallas kernels  84.3 us (98%)
  local copies, waits for them, and re-layouts  1.26 us (1%)
    pallas_call x1, Pallas kernels, body(): pl.pallas_call(kernel, out_shape=jax.ShapeDtypeStruct((EX_DEV, LANE), F32...  84.3 us

profile of v4, /device:TPU:1, one launch (start us, length us, event | category | flops | bytes accessed | tf_op | source)
XLA Modules:
  0.0 85.6 jit_solution(4027016454145883422)
XLA Ops:
  0.0 84.3 %ghost_scores.1 = f32[4,128]{1,0:T(4,128)} custom-call(bf16[128,5120]{1,0:T(8,128)(2,1)} %tx_hbm.1, bf16[6,128,1536]{2,1,0:T(8,128)(2,1)} %bitcast.8, s32[6,128]{1,0:T(8,128)} %bitcast.10, f32[6,128]{1,0:T(8,128)} %bitcast.11, s32[1,128]{1,0:T(1,128)} %bitcast.14, bf16[64,5120]{1,0:T(8,128)(2,1)} %px_hbm.1, bf16[6,64,1536]{2,1,0:T(8,128)(2,1)} %bitcast.9, ...), custom_call_target="tpu_custom_call" | custom-call | flops 16000000000 | bytes 6000000 | tf_op jit(solution)/shard_map/ghost_scores/pallas_call | solution.py:360
  84.3 1.3 %copy.12 = f32[4,128]{1,0:T(4,128)} copy(f32[4,128]{1,0:T(4,128)} %ghost_scores.1) | data formatting | bytes 4096

commit v5 on v3

v5 whole, which is shorter than its diff:
```python
import jax
import jax.numpy as jnp
from jax import lax
from jax.experimental import pallas as pl
from jax.experimental.pallas import tpu as pltpu
from jax.sharding import PartitionSpec as P

MESH = pl.DeviceIdType.MESH
BF = jnp.bfloat16
F32 = jnp.float32

LANE = 128
TOK = 128
PROW = 64
TOP = 6
D = 5120
FF = 1536
NZ = 16
NR = 4
SLOTS = 8
OWN = SLOTS
PEX_ROW = 8
EX_DEV = 4

KQ = FF // 4
KH = FF // 2

XP = D // LANE
GP = KH // LANE
X0 = 1
G0 = X0 + XP
PANELS = G0 + GP * TOP
PARTS = (10, 6)
BASES = (PANELS - NR * PARTS[0], PANELS - NR * sum(PARTS))
PAIRS = SLOTS // 2
LAG = 4


def nt(a, b):
    return lax.dot_general(a, b, (((1,), (1,)), ((), ())), preferred_element_type=F32)


def split(v):
    hi = v.astype(BF)
    return hi, (v - hi.astype(F32)).astype(BF)


def kernel(
    tx_hbm,
    tg_hbm,
    tr_ref,
    tw_ref,
    te_ref,
    px_hbm,
    pg_hbm,
    pr_ref,
    pw_ref,
    pe_ref,
    out_ref,
    slots,
    tx,
    tg,
    tgx,
    away,
    rawg,
    ids,
    marks,
    square,
    pmarks,
    xs,
    near_sum,
    far_sum,
    back_sum,
    acc,
    rbuf,
    lsem,
    zs,
    zr,
    rs,
    rr,
    es,
    er,
    qs,
    qr,
):
    z = lax.axis_index("dp")
    e = lax.axis_index("expert")
    core = e % 2
    xi = (e // 2) % NR
    yi = e // (2 * NR)
    odd = xi % 2

    def at(zz, xx, yy, cc):
        return (zz, (yy * NR + xx) * 2 + cc)

    xr, xl = (xi + 1) % NR, (xi + NR - 1) % NR
    xp, xn = xi + 1 - 2 * odd, (xi + NR - 1 + 2 * odd) % NR
    yr, yl = (yi + 1) % NR, (yi + NR - 1) % NR
    other = at(z, xi, yi, 1 - core)
    mates = (at(z, xp, yi, core), at(z, xn, yi, core))
    across = (at(z, xp, yi, 1 - core), at(z, xn, yi, 1 - core))
    sides = ((at(z, xi, yr, core), at(z, xi, yl, core)), (at(z, xr, yi, core), at(z, xl, yi, core)))
    ranks = (yi, xi)
    above = at((z + 1) % NZ, xi, yi, core)
    below = at((z + NZ - 1) % NZ, xi, yi, core)
    znext = at((z + NZ - 1 + 2 * core) % NZ, xi, yi, core)
    own = jnp.where(core == 0, OWN, 0)
    first = jnp.where(core == 0, 0, 1)

    barrier = pltpu.get_barrier_semaphore()
    greeted = (other, *mates, *across, *sides[0], above, below)
    for who in greeted:
        pl.semaphore_signal(barrier, inc=1, device_id=who, device_id_type=MESH)

    def quarter(i):
        return pl.ds(pl.multiple_of(i * KQ, LANE), KQ)

    mine = (quarter(odd), quarter(3 - odd))
    theirs = (quarter(1 - odd), quarter(2 + odd))
    parts = (pl.ds(0, KQ), pl.ds(KQ, KQ))
    probe_load = [
        pltpu.make_async_copy(pg_hbm.at[:, :, mine[i]], rawg.at[:, :, parts[i]], lsem.at[i]) for i in range(2)
    ]
    for copy in probe_load:
        copy.start()

    @pl.loop(0, XP)
    def _(c):
        cols = pl.ds(pl.multiple_of(c * LANE, LANE), LANE)
        pltpu.make_async_copy(px_hbm.at[:, cols], slots.at[own, X0 + c], lsem.at[2]).start()

    away_load = [pltpu.make_async_copy(tg_hbm.at[:, :, theirs[i]], away.at[i], lsem.at[3 + i]) for i in range(2)]
    grad_load = [
        pltpu.make_async_copy(tg_hbm.at[:, :, mine[i]], tg.at[0, :, :, parts[i]], lsem.at[5 + i]) for i in range(2)
    ]
    for copy in away_load + grad_load:
        copy.start()
    x_load = pltpu.make_async_copy(tx_hbm, tx.at[0], lsem.at[7])
    x_load.start()

    lane = lax.broadcasted_iota(jnp.int32, (1, LANE), 1)
    square[...] = jnp.zeros_like(square)
    square[0:TOP, 0:PROW] = pr_ref[...].astype(F32)
    square[TOP : TOP + 1, 0:PROW] = pe_ref[...].astype(F32)
    square[8 : 8 + TOP, 0:PROW] = pw_ref[...]
    near = square[0:8, :]
    both = near + pltpu.roll(near, PROW, 1)
    pmarks[...] = jnp.zeros_like(pmarks)
    pmarks[0:TOP, :] = both[0:TOP, :]
    pmarks[TOP : TOP + 1, :] = both[TOP : TOP + 1, :] + (z * PEX_ROW).astype(F32)
    slots[own, 0] = pmarks[...].astype(BF)

    turned = jnp.transpose(square[...])
    for copy in probe_load:
        copy.wait()
    for q in range(TOP):
        scale = jnp.broadcast_to(turned[0:PROW, 8 + q : 9 + q], (PROW, LANE))
        for k in range(GP):
            block = rawg[q, :, k * LANE : (k + 1) * LANE].astype(F32)
            slots[own, G0 + k * TOP + q] = (block * scale).astype(BF)
    pltpu.make_async_copy(slots.at[own, pl.ds(X0, XP)], slots.at[own, pl.ds(X0, XP)], lsem.at[2]).wait()

    def remote(src, dst, send, recv, who):
        return pltpu.make_async_remote_copy(
            src_ref=src, dst_ref=dst, send_sem=send, recv_sem=recv, device_id=who, device_id_type=MESH
        )

    def share(slot, axis, who, begin, count):
        return slots.at[slot, pl.ds(BASES[axis] + PARTS[axis] * who + begin, count)]

    def zcopy(src, dst, part):
        if part < 2:
            pick = lambda slot: share(slot, part, ranks[part], 0, PARTS[part])
        else:
            pick = lambda slot: slots.at[slot, pl.ds(0, BASES[1])]
        return remote(pick(src), pick(dst), zs.at[dst, part], zr.at[dst, part], znext)

    def ring(slot, axis, kind, landing=False):
        size = PARTS[axis]
        who = (0, 0, NR - 1, 1)[kind] + ((NR - 1, 1)[kind % 2] if landing else 0)
        begin, count = ((0, size), (0, size), (0, size // 2), (size // 2, size - size // 2))[kind]
        region = share(slot, axis, (ranks[axis] + who) % NR, begin, count)
        return remote(region, region, rs.at[slot, axis, kind], rr.at[slot, axis, kind], sides[axis][kind % 2])

    pl.semaphore_wait(barrier, len(greeted))
    for part in range(3):
        zcopy(own, first, part).start()

    marks[0] = jnp.zeros((16, LANE), F32)
    marks[0, 0:TOP, :] = tr_ref[...].astype(F32)
    marks[0, TOP : TOP + 1, :] = te_ref[...].astype(F32)
    square[...] = jnp.zeros_like(square)
    square[0:TOP, :] = tr_ref[...].astype(F32)
    square[8 : 8 + TOP, :] = tw_ref[...]
    turned = jnp.transpose(square[...])

    def scale_train(ref, panels):
        for r in range(TOP):
            scale = jnp.broadcast_to(turned[:, 8 + r : 9 + r], (TOK, LANE))

            @pl.loop(0, panels)
            def _(k):
                cols = pl.ds(pl.multiple_of(k * LANE, LANE), LANE)
                ref[r, :, cols] = (ref[r, :, cols].astype(F32) * scale).astype(BF)

    def spread(group):
        square[0:16, :] = marks[group]
        columns = jnp.transpose(square[...])
        for r in range(TOP):
            ids[group, r] = jnp.broadcast_to(columns[:, r : r + 1], (TOK, LANE))

    def swap(src, dst, which, who):
        return remote(src, dst, es.at[which], er.at[which], who)

    swaps = (
        swap(marks.at[0], marks.at[1], 0, other),
        swap(marks.at[0], marks.at[2], 1, mates[0]),
        swap(marks.at[0], marks.at[3], 2, across[0]),
        swap(marks.at[0], marks.at[4], 3, mates[1]),
        swap(marks.at[0], marks.at[5], 4, across[1]),
        swap(away.at[0], tgx.at[0], 5, mates[0]),
        swap(away.at[1], tgx.at[2], 6, mates[1]),
        swap(tx.at[0], tx.at[1], 7, other),
        swap(tg.at[0], tg.at[1], 8, other),
        swap(tgx.at[0], tgx.at[1], 9, other),
        swap(tgx.at[2], tgx.at[3], 10, other),
    )
    for i in range(2):
        away_load[i].wait()
        scale_train(away.at[i], KQ // LANE)
        swaps[5 + i].start()
    for which in range(5):
        swaps[which].start()
    x_load.wait()
    swaps[7].start()
    for copy in grad_load:
        copy.wait()
    scale_train(tg.at[0], GP)
    swaps[8].start()
    spread(0)

    def meet_core():
        swaps[0].wait_recv()
        spread(1)
        swaps[7].wait_recv()
        swaps[8].wait_recv()

    def meet_mates():
        for i in range(2):
            swaps[5 + i].wait_recv()
            swaps[9 + i].start()
        for group in range(2, 6):
            swaps[group - 1].wait_recv()
            spread(group)

    def feature_gram(pair):
        px = jnp.concatenate(
            [jnp.concatenate([slots[2 * pair + i, X0 + c] for c in range(XP)], axis=1) for i in range(2)], axis=0
        )
        xs[pair] = nt(tx[...].reshape(2 * TOK, D), px).reshape(2, TOK, LANE)

    def route_gram(pair, lhs, group, panels):
        info = [slots[2 * pair + i, 0, 0:16, :].astype(F32) for i in range(2)]
        info = jnp.where(lane < PROW, info[0], info[1])
        pg = jnp.concatenate(
            [
                jnp.concatenate(
                    [slots[2 * pair + i, G0 + k * TOP + q] for q in range(TOP) for i in range(2)], axis=0
                )
                for k in panels
            ],
            axis=1,
        )
        gram = nt(lhs.reshape(TOP * TOK, len(panels) * LANE), pg)
        total = jnp.zeros((TOK, LANE), F32)
        for r in range(TOP):
            who = ids[group, r]
            for q in range(TOP):
                part = gram[r * TOK : (r + 1) * TOK, q * LANE : (q + 1) * LANE]
                total = total + jnp.where(who == info[q : q + 1, :], part, 0.0)
        return total

    def give_back(pair, i):
        return remote(far_sum.at[pair, i], back_sum.at[pair, i], qs.at[pair, i], qr.at[pair, i], mates[i])

    def own_tokens(pair):
        for h in range(2):
            near_sum[pair, h] = route_gram(pair, tg[h], h, range(GP))

    def mate_tokens(pair, i):
        for h in range(2):
            panels = range(i * GP // 2, (i + 1) * GP // 2)
            far_sum[pair, i, h] = route_gram(pair, tgx[2 * i + h], 2 + 2 * i + h, panels).astype(BF)
        give_back(pair, i).start()

    def taken(j):
        return (core == 0) | (j >= 1)

    @pl.loop(0, SLOTS + LAG)
    def _(j):
        fresh = (j < SLOTS) & taken(j)
        ready = j >= LAG
        since = jnp.maximum(j - LAG, 0)
        pair = since // 2
        at_home = (since % 2 == 0) != (pair == PAIRS - 1)

        def pass_on(part):
            @pl.when(fresh)
            def _():
                zcopy(j, j, part).wait_recv()

                @pl.when(j < SLOTS - 1)
                def _():
                    zcopy(j, jnp.minimum(j + 1, SLOTS - 1), part).start()

                if part < 2:
                    ring(j, part, 0).start()
                    ring(j, part, 1).start()

        pass_on(0)

        @pl.when(j == LAG + 1)
        def _():
            swaps[9].wait_recv()
            swaps[10].wait_recv()

        pl.when(ready & at_home)(lambda: feature_gram(pair))
        pl.when(ready & ~at_home)(lambda: mate_tokens(pair, 0))
        pass_on(1)
        pl.when(ready & at_home)(lambda: own_tokens(pair))
        pl.when(ready & ~at_home)(lambda: mate_tokens(pair, 1))
        pass_on(2)
        pl.when(j == LAG - 1)(meet_core)

        @pl.when((j >= 1) & (j < SLOTS + 1) & taken(j - 1))
        def _():
            slot = jnp.maximum(j - 1, 0)
            for kind in range(2):
                for axis in range(2):
                    ring(slot, axis, kind, True).wait_recv()
                    ring(slot, axis, kind + 2).start()

        pl.when(j == LAG)(meet_mates)

        @pl.when((j >= 2) & (j < SLOTS + 2) & taken(j - 2))
        def _():
            slot = jnp.maximum(j - 2, 0)
            for kind in range(2, 4):
                for axis in range(2):
                    ring(slot, axis, kind, True).wait_recv()

    rows = lax.broadcasted_iota(jnp.int32, (LANE, LANE), 0).astype(F32)
    rows16 = lax.broadcasted_iota(jnp.int32, (16, TOK), 0).astype(F32)
    owners, values = [], ([], [])
    for pair in range(PAIRS):
        info = [slots[2 * pair + i, 0, 0:16, :].astype(F32) for i in range(2)]
        info = jnp.where(lane < PROW, info[0], info[1])
        owners.append((rows == info[TOP : TOP + 1, :]).astype(BF))
        for i in range(2):
            give_back(pair, i).wait_recv()
        for h in range(2):
            back = back_sum[pair, 0, h].astype(F32) + back_sum[pair, 1, h].astype(F32)
            values[h].append((near_sum[pair, h] + back) * xs[pair, h])
    owners = jnp.concatenate(owners, axis=1)
    sums = []
    for h in range(2):
        hi, lo = split(jnp.concatenate(values[h], axis=1))
        examples = (rows16 == marks[h, TOP : TOP + 1, :]).astype(BF)
        part = jnp.dot(examples, hi, preferred_element_type=F32) + jnp.dot(examples, lo, preferred_element_type=F32)
        sums.append(part[0:8, :])
    hi, lo = split(jnp.concatenate(sums, axis=0))
    acc[...] = nt(hi, owners) + nt(lo, owners)

    last = swap(acc.at[pl.ds(8, 8)], rbuf, 11, other)
    last.start()
    last.wait_recv()
    out_ref[...] = acc[0:EX_DEV, :] + rbuf[0:EX_DEV, :]

    last.wait_send()
    for copy in swaps:
        copy.wait_send()

    @pl.loop(0, PAIRS)
    def _(pair):
        for i in range(2):
            give_back(pair, i).wait_send()

    @pl.loop(0, SLOTS)
    def _(j):
        @pl.when(taken(j))
        def _():
            for part in range(3):
                zcopy(j, j, part).wait_send()
            for axis in range(2):
                for kind in range(4):
                    ring(j, axis, kind).wait_send()


def body(
    train_x,
    train_grad,
    train_routes,
    train_weight,
    train_example,
    probe_x,
    probe_grad,
    probe_routes,
    probe_weight,
    probe_example,
):
    hbm = pl.BlockSpec(memory_space=pl.ANY)
    vmem = pl.BlockSpec(memory_space=pltpu.VMEM)
    dma = pltpu.SemaphoreType.DMA
    return pl.pallas_call(
        kernel,
        out_shape=jax.ShapeDtypeStruct((EX_DEV, LANE), F32),
        in_specs=[hbm, hbm, vmem, vmem, vmem, hbm, hbm, vmem, vmem, vmem],
        out_specs=vmem,
        scratch_shapes=[
            pltpu.VMEM((SLOTS + 1, PANELS, PROW, LANE), BF),
            pltpu.VMEM((2, TOK, D), BF),
            pltpu.VMEM((2, TOP, TOK, KH), BF),
            pltpu.VMEM((4, TOP, TOK, KQ), BF),
            pltpu.VMEM((2, TOP, TOK, KQ), BF),
            pltpu.VMEM((TOP, PROW, KH), BF),
            pltpu.VMEM((6, TOP, TOK, LANE), F32),
            pltpu.VMEM((6, 16, LANE), F32),
            pltpu.VMEM((LANE, LANE), F32),
            pltpu.VMEM((PROW, LANE), F32),
            pltpu.VMEM((PAIRS, 2, TOK, LANE), F32),
            pltpu.VMEM((PAIRS, 2, TOK, LANE), F32),
            pltpu.VMEM((PAIRS, 2, 2, TOK, LANE), BF),
            pltpu.VMEM((PAIRS, 2, 2, TOK, LANE), BF),
            pltpu.VMEM((16, LANE), F32),
            pltpu.VMEM((8, LANE), F32),
            dma((8,)),
            dma((SLOTS, 3)),
            dma((SLOTS, 3)),
            dma((SLOTS, 2, 4)),
            dma((SLOTS, 2, 4)),
            dma((12,)),
            dma((12,)),
            dma((PAIRS, 2)),
            dma((PAIRS, 2)),
        ],
        compiler_params=pltpu.CompilerParams(
            collective_id=0, has_side_effects=True, vmem_limit_bytes=56 * 1024 * 1024
        ),
        cost_estimate=pl.CostEstimate(flops=16_000_000_000, bytes_accessed=6_000_000, transcendentals=0),
        name="ghost_scores",
    )(
        train_x,
        jnp.transpose(train_grad, (1, 0, 2)),
        train_routes.T,
        train_weight.T,
        train_example[None, :],
        probe_x,
        jnp.transpose(probe_grad, (1, 0, 2)),
        probe_routes.T,
        probe_weight.T,
        probe_example[None, :],
    )


def solution(mesh):
    in_specs = (
        P(("dp", "expert"), None),
        P(("dp", "expert"), None, None),
        P(("dp", "expert"), None),
        P(("dp", "expert"), None),
        P(("dp", "expert")),
        P("dp", None),
        P("dp", None, None),
        P("dp", None),
        P("dp", None),
        P("dp"),
    )
    out_specs = P(("dp", "expert"), None)
    return jax.shard_map(body, mesh=mesh, in_specs=in_specs, out_specs=out_specs, check_vma=False)
```

time: 94.6 us -> 82 us (0.87)
  Pallas kernels: 93.2 us -> 80.6 us
    pallas_call x1, Pallas kernels: 93.2 us -> 80.6 us  [body(): pl.pallas_call(kernel, out_shape=jax.ShapeDtypeStruct((EX_DEV, LANE), F32...]
where the time goes in v5:
time: 82 us; the launch traced here: 81.9 us
  Pallas kernels  80.6 us (98%)
  local copies, waits for them, and re-layouts  1.26 us (2%)
    pallas_call x1, Pallas kernels, body(): pl.pallas_call(kernel, out_shape=jax.ShapeDtypeStruct((EX_DEV, LANE), F32...  80.6 us

profile of v5, /device:TPU:1, one launch (start us, length us, event | category | flops | bytes accessed | tf_op | source)
XLA Modules:
  0.0 81.9 jit_solution(7245760405358314828)
XLA Ops:
  0.0 80.6 %ghost_scores.1 = f32[4,128]{1,0:T(4,128)} custom-call(bf16[128,5120]{1,0:T(8,128)(2,1)} %tx_hbm.1, bf16[6,128,1536]{2,1,0:T(8,128)(2,1)} %bitcast.8, s32[6,128]{1,0:T(8,128)} %bitcast.10, f32[6,128]{1,0:T(8,128)} %bitcast.11, s32[1,128]{1,0:T(1,128)} %bitcast.14, bf16[64,5120]{1,0:T(8,128)(2,1)} %px_hbm.1, bf16[6,64,1536]{2,1,0:T(8,128)(2,1)} %bitcast.9, ...), custom_call_target="tpu_custom_call" | custom-call | flops 16000000000 | bytes 6000000 | tf_op jit(solution)/shard_map/ghost_scores/pallas_call | solution.py:414
  80.6 1.3 %copy.12 = f32[4,128]{1,0:T(4,128)} copy(f32[4,128]{1,0:T(4,128)} %ghost_scores.1) | data formatting | bytes 4096

commit v6 on v5

--- a/solution.py
+++ b/solution.py
@@ -32,8 +32,8 @@
 PANELS = G0 + GP * TOP
 PARTS = (10, 6)
 BASES = (PANELS - NR * PARTS[0], PANELS - NR * sum(PARTS))
-PAIRS = SLOTS // 2
-LAG = 4
+PAIRS = 3
+UNITS = PAIRS + 2
 
 
 def nt(a, b):
@@ -186,6 +186,7 @@
     for part in range(3):
         zcopy(own, first, part).start()
 
+    acc[...] = jnp.zeros_like(acc)
     marks[0] = jnp.zeros((16, LANE), F32)
     marks[0, 0:TOP, :] = tr_ref[...].astype(F32)
     marks[0, TOP : TOP + 1, :] = te_ref[...].astype(F32)
@@ -253,20 +254,35 @@
             swaps[group - 1].wait_recv()
             spread(group)
 
-    def feature_gram(pair):
-        px = jnp.concatenate(
-            [jnp.concatenate([slots[2 * pair + i, X0 + c] for c in range(XP)], axis=1) for i in range(2)], axis=0
-        )
-        xs[pair] = nt(tx[...].reshape(2 * TOK, D), px).reshape(2, TOK, LANE)
-
-    def route_gram(pair, lhs, group, panels):
-        info = [slots[2 * pair + i, 0, 0:16, :].astype(F32) for i in range(2)]
-        info = jnp.where(lane < PROW, info[0], info[1])
+    def planes_of(unit, count):
+        return [2 * unit, 2 * unit + 1] if count == 2 else [unit + PAIRS]
+
+    def marks_of(unit, count):
+        info = [slots[slot, 0, 0:16, :].astype(F32) for slot in planes_of(unit, count)]
+        if count == 2:
+            info = jnp.where(lane < PROW, info[0], info[1])
+            rows = [info[q : q + 1, :] for q in range(TOP)]
+        else:
+            info = info[0]
+            rows = [
+                jnp.where(lane < PROW, info[q : q + 1, :], info[q + 1 : q + 2, :]) for q in range(0, TOP, 2)
+            ]
+        return rows, info[TOP : TOP + 1, :]
+
+    def feature_gram(unit, count):
+        planes = planes_of(unit, count)
+        px = [jnp.concatenate([slots[slot, X0 + c] for c in range(XP)], axis=1) for slot in planes]
+        gram = nt(tx[...].reshape(2 * TOK, D), jnp.concatenate(px * (2 // count), axis=0))
+        if count == 1:
+            gram = jnp.where(lane < PROW, gram, 0.0)
+        xs[unit] = gram.reshape(2, TOK, LANE)
+
+    def route_gram(unit, count, lhs, group, panels):
+        rows, _ = marks_of(unit, count)
+        planes = planes_of(unit, count)
         pg = jnp.concatenate(
             [
-                jnp.concatenate(
-                    [slots[2 * pair + i, G0 + k * TOP + q] for q in range(TOP) for i in range(2)], axis=0
-                )
+                jnp.concatenate([slots[slot, G0 + k * TOP + q] for q in range(TOP) for slot in planes], axis=0)
                 for k in panels
             ],
             axis=1,
@@ -275,37 +291,73 @@
         total = jnp.zeros((TOK, LANE), F32)
         for r in range(TOP):
             who = ids[group, r]
-            for q in range(TOP):
+            for q, row in enumerate(rows):
                 part = gram[r * TOK : (r + 1) * TOK, q * LANE : (q + 1) * LANE]
-                total = total + jnp.where(who == info[q : q + 1, :], part, 0.0)
+                total = total + jnp.where(who == row, part, 0.0)
+        if count == 1:
+            total = total + pltpu.roll(total, PROW, 1)
         return total
 
-    def give_back(pair, i):
-        return remote(far_sum.at[pair, i], back_sum.at[pair, i], qs.at[pair, i], qr.at[pair, i], mates[i])
-
-    def own_tokens(pair):
+    def give_back(unit, i):
+        return remote(far_sum.at[unit, i], back_sum.at[unit, i], qs.at[unit, i], qr.at[unit, i], mates[i])
+
+    def own_tokens(unit, count):
+        feature_gram(unit, count)
         for h in range(2):
-            near_sum[pair, h] = route_gram(pair, tg[h], h, range(GP))
-
-    def mate_tokens(pair, i):
+            near_sum[unit, h] = route_gram(unit, count, tg[h], h, range(GP))
+
+    def mate_tokens(unit, count, i):
         for h in range(2):
             panels = range(i * GP // 2, (i + 1) * GP // 2)
-            far_sum[pair, i, h] = route_gram(pair, tgx[2 * i + h], 2 + 2 * i + h, panels).astype(BF)
-        give_back(pair, i).start()
+            part = route_gram(unit, count, tgx[2 * i + h], 2 + 2 * i + h, panels)
+            far_sum[unit, i, h] = part.astype(BF)
+        give_back(unit, i).start()
+
+    def add_scores(units):
+        square_rows = lax.broadcasted_iota(jnp.int32, (LANE, LANE), 0).astype(F32)
+        rows16 = lax.broadcasted_iota(jnp.int32, (16, TOK), 0).astype(F32)
+        owners, values = [], ([], [])
+        for unit in units:
+            _, owner = marks_of(*((unit, 2) if unit < PAIRS else (unit, 1)))
+            owners.append((square_rows == owner).astype(BF))
+            for i in range(2):
+                give_back(unit, i).wait_recv()
+            for h in range(2):
+                back = back_sum[unit, 0, h].astype(F32) + back_sum[unit, 1, h].astype(F32)
+                values[h].append((near_sum[unit, h] + back) * xs[unit, h])
+        owners = jnp.concatenate(owners, axis=1)
+        sums = []
+        for h in range(2):
+            hi, lo = split(jnp.concatenate(values[h], axis=1))
+            examples = (rows16 == marks[h, TOP : TOP + 1, :]).astype(BF)
+            part = jnp.dot(examples, hi, preferred_element_type=F32)
+            part = part + jnp.dot(examples, lo, preferred_element_type=F32)
+            sums.append(part[0:8, :])
+        hi, lo = split(jnp.concatenate(sums, axis=0))
+        acc[...] += nt(hi, owners) + nt(lo, owners)
 
     def taken(j):
         return (core == 0) | (j >= 1)
 
-    @pl.loop(0, SLOTS + LAG)
+    def hop(slot):
+        for kind in range(2):
+            for axis in range(2):
+                ring(slot, axis, kind, True).wait_recv()
+                ring(slot, axis, kind + 2).start()
+
+    def filled(slot):
+        for kind in range(2, 4):
+            for axis in range(2):
+                ring(slot, axis, kind, True).wait_recv()
+
+    @pl.loop(0, SLOTS)
     def _(j):
-        fresh = (j < SLOTS) & taken(j)
-        ready = j >= LAG
-        since = jnp.maximum(j - LAG, 0)
-        pair = since // 2
-        at_home = (since % 2 == 0) != (pair == PAIRS - 1)
+        home = (j >= 3) & (j % 2 == 1)
+        pair = jnp.clip((j - 3) // 2, 0, PAIRS - 1)
+        visit = ((j >= 4) & (j % 2 == 0)) | (j == SLOTS - 1)
 
         def pass_on(part):
-            @pl.when(fresh)
+            @pl.when(taken(j))
             def _():
                 zcopy(j, j, part).wait_recv()
 
@@ -318,58 +370,32 @@
                     ring(j, part, 1).start()
 
         pass_on(0)
-
-        @pl.when(j == LAG + 1)
+        pass_on(1)
+        pl.when((j >= 1) & taken(j - 1))(lambda: hop(jnp.maximum(j - 1, 0)))
+        pl.when((j >= 2) & taken(j - 2))(lambda: filled(jnp.maximum(j - 2, 0)))
+
+        @pl.when(j == 4)
         def _():
             swaps[9].wait_recv()
             swaps[10].wait_recv()
 
-        pl.when(ready & at_home)(lambda: feature_gram(pair))
-        pl.when(ready & ~at_home)(lambda: mate_tokens(pair, 0))
-        pass_on(1)
-        pl.when(ready & at_home)(lambda: own_tokens(pair))
-        pl.when(ready & ~at_home)(lambda: mate_tokens(pair, 1))
+        pl.when(home)(lambda: own_tokens(pair, 2))
+        pl.when(visit)(lambda: mate_tokens(pair, 2, 0))
         pass_on(2)
-        pl.when(j == LAG - 1)(meet_core)
-
-        @pl.when((j >= 1) & (j < SLOTS + 1) & taken(j - 1))
-        def _():
-            slot = jnp.maximum(j - 1, 0)
-            for kind in range(2):
-                for axis in range(2):
-                    ring(slot, axis, kind, True).wait_recv()
-                    ring(slot, axis, kind + 2).start()
-
-        pl.when(j == LAG)(meet_mates)
-
-        @pl.when((j >= 2) & (j < SLOTS + 2) & taken(j - 2))
-        def _():
-            slot = jnp.maximum(j - 2, 0)
-            for kind in range(2, 4):
-                for axis in range(2):
-                    ring(slot, axis, kind, True).wait_recv()
-
-    rows = lax.broadcasted_iota(jnp.int32, (LANE, LANE), 0).astype(F32)
-    rows16 = lax.broadcasted_iota(jnp.int32, (16, TOK), 0).astype(F32)
-    owners, values = [], ([], [])
-    for pair in range(PAIRS):
-        info = [slots[2 * pair + i, 0, 0:16, :].astype(F32) for i in range(2)]
-        info = jnp.where(lane < PROW, info[0], info[1])
-        owners.append((rows == info[TOP : TOP + 1, :]).astype(BF))
-        for i in range(2):
-            give_back(pair, i).wait_recv()
-        for h in range(2):
-            back = back_sum[pair, 0, h].astype(F32) + back_sum[pair, 1, h].astype(F32)
-            values[h].append((near_sum[pair, h] + back) * xs[pair, h])
-    owners = jnp.concatenate(owners, axis=1)
-    sums = []
-    for h in range(2):
-        hi, lo = split(jnp.concatenate(values[h], axis=1))
-        examples = (rows16 == marks[h, TOP : TOP + 1, :]).astype(BF)
-        part = jnp.dot(examples, hi, preferred_element_type=F32) + jnp.dot(examples, lo, preferred_element_type=F32)
-        sums.append(part[0:8, :])
-    hi, lo = split(jnp.concatenate(sums, axis=0))
-    acc[...] = nt(hi, owners) + nt(lo, owners)
+        pl.when(visit)(lambda: mate_tokens(pair, 2, 1))
+        pl.when(j == 2)(meet_core)
+        pl.when(j == 3)(meet_mates)
+
+    @pl.loop(PAIRS, UNITS)
+    def _(unit):
+        filled(unit + PAIRS)
+        mate_tokens(unit, 1, 0)
+        pl.when(unit == PAIRS)(lambda: hop(SLOTS - 1))
+        mate_tokens(unit, 1, 1)
+        own_tokens(unit, 1)
+        pl.when(unit == PAIRS)(lambda: add_scores(range(PAIRS + 1)))
+
+    add_scores([UNITS - 1])
 
     last = swap(acc.at[pl.ds(8, 8)], rbuf, 11, other)
     last.start()
@@ -380,10 +406,10 @@
     for copy in swaps:
         copy.wait_send()
 
-    @pl.loop(0, PAIRS)
-    def _(pair):
+    @pl.loop(0, UNITS)
+    def _(unit):
         for i in range(2):
-            give_back(pair, i).wait_send()
+            give_back(unit, i).wait_send()
 
     @pl.loop(0, SLOTS)
     def _(j):
@@ -427,10 +453,10 @@
             pltpu.VMEM((6, 16, LANE), F32),
             pltpu.VMEM((LANE, LANE), F32),
             pltpu.VMEM((PROW, LANE), F32),
-            pltpu.VMEM((PAIRS, 2, TOK, LANE), F32),
-            pltpu.VMEM((PAIRS, 2, TOK, LANE), F32),
-            pltpu.VMEM((PAIRS, 2, 2, TOK, LANE), BF),
-            pltpu.VMEM((PAIRS, 2, 2, TOK, LANE), BF),
+            pltpu.VMEM((UNITS, 2, TOK, LANE), F32),
+            pltpu.VMEM((UNITS, 2, TOK, LANE), F32),
+            pltpu.VMEM((UNITS, 2, 2, TOK, LANE), BF),
+            pltpu.VMEM((UNITS, 2, 2, TOK, LANE), BF),
             pltpu.VMEM((16, LANE), F32),
             pltpu.VMEM((8, LANE), F32),
             dma((8,)),
@@ -440,8 +466,8 @@
             dma((SLOTS, 2, 4)),
             dma((12,)),
             dma((12,)),
-            dma((PAIRS, 2)),
-            dma((PAIRS, 2)),
+            dma((UNITS, 2)),
+            dma((UNITS, 2)),
         ],
         compiler_params=pltpu.CompilerParams(
             collective_id=0, has_side_effects=True, vmem_limit_bytes=56 * 1024 * 1024

time: 82 us -> 85.9 us (1.048)
  Pallas kernels: 80.6 us -> 84.4 us
    pallas_call x1, Pallas kernels: 80.6 us -> 84.4 us  [body(): pl.pallas_call(kernel, out_shape=jax.ShapeDtypeStruct((EX_DEV, LANE), F32...]
where the time goes in v6:
time: 85.9 us; the launch traced here: 85.7 us
  Pallas kernels  84.4 us (98%)
  local copies, waits for them, and re-layouts  1.26 us (1%)
    pallas_call x1, Pallas kernels, body(): pl.pallas_call(kernel, out_shape=jax.ShapeDtypeStruct((EX_DEV, LANE), F32...  84.4 us

profile of v6, /device:TPU:1, one launch (start us, length us, event | category | flops | bytes accessed | tf_op | source)
XLA Modules:
  0.0 85.7 jit_solution(15497431585745632433)
XLA Ops:
  0.0 84.4 %ghost_scores.1 = f32[4,128]{1,0:T(4,128)} custom-call(bf16[128,5120]{1,0:T(8,128)(2,1)} %tx_hbm.1, bf16[6,128,1536]{2,1,0:T(8,128)(2,1)} %bitcast.8, s32[6,128]{1,0:T(8,128)} %bitcast.10, f32[6,128]{1,0:T(8,128)} %bitcast.11, s32[1,128]{1,0:T(1,128)} %bitcast.14, bf16[64,5120]{1,0:T(8,128)(2,1)} %px_hbm.1, bf16[6,64,1536]{2,1,0:T(8,128)(2,1)} %bitcast.9, ...), custom_call_target="tpu_custom_call" | custom-call | flops 16000000000 | bytes 6000000 | tf_op jit(solution)/shard_map/ghost_scores/pallas_call | solution.py:440
  84.4 1.3 %copy.12 = f32[4,128]{1,0:T(4,128)} copy(f32[4,128]{1,0:T(4,128)} %ghost_scores.1) | data formatting | bytes 4096

commit v7 on v5

--- a/solution.py
+++ b/solution.py
@@ -32,8 +32,8 @@
 PANELS = G0 + GP * TOP
 PARTS = (10, 6)
 BASES = (PANELS - NR * PARTS[0], PANELS - NR * sum(PARTS))
-PAIRS = SLOTS // 2
-LAG = 4
+LAG = 2
+MEET = 4
 
 
 def nt(a, b):
@@ -62,11 +62,12 @@
     tg,
     tgx,
     away,
+    rawx,
+    rawt,
+    rawa,
     rawg,
-    ids,
     marks,
     square,
-    pmarks,
     xs,
     near_sum,
     far_sum,
@@ -129,28 +130,23 @@
         cols = pl.ds(pl.multiple_of(c * LANE, LANE), LANE)
         pltpu.make_async_copy(px_hbm.at[:, cols], slots.at[own, X0 + c], lsem.at[2]).start()
 
-    away_load = [pltpu.make_async_copy(tg_hbm.at[:, :, theirs[i]], away.at[i], lsem.at[3 + i]) for i in range(2)]
+    away_load = [pltpu.make_async_copy(tg_hbm.at[:, :, theirs[i]], rawa.at[i], lsem.at[3 + i]) for i in range(2)]
     grad_load = [
-        pltpu.make_async_copy(tg_hbm.at[:, :, mine[i]], tg.at[0, :, :, parts[i]], lsem.at[5 + i]) for i in range(2)
+        pltpu.make_async_copy(tg_hbm.at[:, :, mine[i]], rawt.at[:, :, parts[i]], lsem.at[5 + i]) for i in range(2)
     ]
     for copy in away_load + grad_load:
         copy.start()
-    x_load = pltpu.make_async_copy(tx_hbm, tx.at[0], lsem.at[7])
+    x_load = pltpu.make_async_copy(tx_hbm, rawx, lsem.at[7])
     x_load.start()
 
     lane = lax.broadcasted_iota(jnp.int32, (1, LANE), 1)
     square[...] = jnp.zeros_like(square)
     square[0:TOP, 0:PROW] = pr_ref[...].astype(F32)
-    square[TOP : TOP + 1, 0:PROW] = pe_ref[...].astype(F32)
+    square[TOP : TOP + 1, 0:PROW] = pe_ref[...].astype(F32) + (z * PEX_ROW).astype(F32)
     square[8 : 8 + TOP, 0:PROW] = pw_ref[...]
-    near = square[0:8, :]
-    both = near + pltpu.roll(near, PROW, 1)
-    pmarks[...] = jnp.zeros_like(pmarks)
-    pmarks[0:TOP, :] = both[0:TOP, :]
-    pmarks[TOP : TOP + 1, :] = both[TOP : TOP + 1, :] + (z * PEX_ROW).astype(F32)
-    slots[own, 0] = pmarks[...].astype(BF)
-
     turned = jnp.transpose(square[...])
+    slots[own, 0] = jnp.where(lane <= TOP, turned[0:PROW, :], 0.0).astype(BF)
+
     for copy in probe_load:
         copy.wait()
     for q in range(TOP):
@@ -186,28 +182,29 @@
     for part in range(3):
         zcopy(own, first, part).start()
 
+    acc[...] = jnp.zeros_like(acc)
     marks[0] = jnp.zeros((16, LANE), F32)
     marks[0, 0:TOP, :] = tr_ref[...].astype(F32)
     marks[0, TOP : TOP + 1, :] = te_ref[...].astype(F32)
     square[...] = jnp.zeros_like(square)
-    square[0:TOP, :] = tr_ref[...].astype(F32)
-    square[8 : 8 + TOP, :] = tw_ref[...]
-    turned = jnp.transpose(square[...])
-
-    def scale_train(ref, panels):
+    square[0:TOP, :] = tw_ref[...]
+
+    def turn_grad(src, dst, panels):
+        weights = jnp.transpose(square[...])
         for r in range(TOP):
-            scale = jnp.broadcast_to(turned[:, 8 + r : 9 + r], (TOK, LANE))
+            scale = jnp.broadcast_to(weights[:, r : r + 1], (TOK, LANE))
 
             @pl.loop(0, panels)
             def _(k):
                 cols = pl.ds(pl.multiple_of(k * LANE, LANE), LANE)
-                ref[r, :, cols] = (ref[r, :, cols].astype(F32) * scale).astype(BF)
-
-    def spread(group):
-        square[0:16, :] = marks[group]
-        columns = jnp.transpose(square[...])
-        for r in range(TOP):
-            ids[group, r] = jnp.broadcast_to(columns[:, r : r + 1], (TOK, LANE))
+                block = (src[r, :, cols].astype(F32) * scale).astype(BF).astype(F32)
+                dst[cols, r * TOK : (r + 1) * TOK] = jnp.transpose(block).astype(BF)
+
+    def turn_x():
+        @pl.loop(0, XP)
+        def _(k):
+            cols = pl.ds(pl.multiple_of(k * LANE, LANE), LANE)
+            tx[0, cols, :] = jnp.transpose(rawx[:, cols].astype(F32)).astype(BF)
 
     def swap(src, dst, which, who):
         return remote(src, dst, es.at[which], er.at[which], who)
@@ -227,21 +224,24 @@
     )
     for i in range(2):
         away_load[i].wait()
-        scale_train(away.at[i], KQ // LANE)
+        turn_grad(rawa.at[i], away.at[i], KQ // LANE)
         swaps[5 + i].start()
     for which in range(5):
         swaps[which].start()
-    x_load.wait()
-    swaps[7].start()
-    for copy in grad_load:
-        copy.wait()
-    scale_train(tg.at[0], GP)
-    swaps[8].start()
-    spread(0)
+
+    def give_core_grad():
+        for copy in grad_load:
+            copy.wait()
+        turn_grad(rawt, tg.at[0], GP)
+        swaps[8].start()
+
+    def give_core_x():
+        x_load.wait()
+        turn_x()
+        swaps[7].start()
 
     def meet_core():
         swaps[0].wait_recv()
-        spread(1)
         swaps[7].wait_recv()
         swaps[8].wait_recv()
 
@@ -249,49 +249,64 @@
         for i in range(2):
             swaps[5 + i].wait_recv()
             swaps[9 + i].start()
-        for group in range(2, 6):
-            swaps[group - 1].wait_recv()
-            spread(group)
-
-    def feature_gram(pair):
-        px = jnp.concatenate(
-            [jnp.concatenate([slots[2 * pair + i, X0 + c] for c in range(XP)], axis=1) for i in range(2)], axis=0
+        for which in range(1, 5):
+            swaps[which].wait_recv()
+
+    def feature_gram(slot):
+        px = jnp.concatenate([slots[slot, X0 + c] for c in range(XP)], axis=1)
+        gram = jnp.dot(px, jnp.concatenate([tx[0], tx[1]], axis=1), preferred_element_type=F32)
+        for h in range(2):
+            xs[slot, h] = gram[:, h * TOK : (h + 1) * TOK]
+
+    def route_gram(slot, rhs, group, panels):
+        info = slots[slot, 0].astype(F32)
+        pg = jnp.concatenate(
+            [slots[slot, G0 + k * TOP : G0 + (k + 1) * TOP].reshape(TOP * PROW, LANE) for k in panels], axis=1
         )
-        xs[pair] = nt(tx[...].reshape(2 * TOK, D), px).reshape(2, TOK, LANE)
-
-    def route_gram(pair, lhs, group, panels):
-        info = [slots[2 * pair + i, 0, 0:16, :].astype(F32) for i in range(2)]
-        info = jnp.where(lane < PROW, info[0], info[1])
-        pg = jnp.concatenate(
-            [
-                jnp.concatenate(
-                    [slots[2 * pair + i, G0 + k * TOP + q] for q in range(TOP) for i in range(2)], axis=0
-                )
-                for k in panels
-            ],
-            axis=1,
-        )
-        gram = nt(lhs.reshape(TOP * TOK, len(panels) * LANE), pg)
-        total = jnp.zeros((TOK, LANE), F32)
-        for r in range(TOP):
-            who = ids[group, r]
-            for q in range(TOP):
-                part = gram[r * TOK : (r + 1) * TOK, q * LANE : (q + 1) * LANE]
-                total = total + jnp.where(who == info[q : q + 1, :], part, 0.0)
+        gram = jnp.dot(pg, rhs, preferred_element_type=F32)
+        total = jnp.zeros((PROW, LANE), F32)
+        for q in range(TOP):
+            who = jnp.broadcast_to(info[:, q : q + 1], (PROW, LANE))
+            for r in range(TOP):
+                part = gram[q * PROW : (q + 1) * PROW, r * TOK : (r + 1) * TOK]
+                total = total + jnp.where(who == marks[group, r : r + 1, :], part, 0.0)
         return total
 
-    def give_back(pair, i):
-        return remote(far_sum.at[pair, i], back_sum.at[pair, i], qs.at[pair, i], qr.at[pair, i], mates[i])
-
-    def own_tokens(pair):
+    def give_back(slot, i):
+        return remote(far_sum.at[slot, i], back_sum.at[slot, i], qs.at[slot, i], qr.at[slot, i], mates[i])
+
+    def own_tokens(slot):
+        feature_gram(slot)
         for h in range(2):
-            near_sum[pair, h] = route_gram(pair, tg[h], h, range(GP))
-
-    def mate_tokens(pair, i):
+            near_sum[slot, h] = route_gram(slot, tg[h], h, range(GP))
+
+    def mate_tokens(slot):
+        for i in range(2):
+            panels = range(i * GP // 2, (i + 1) * GP // 2)
+            for h in range(2):
+                far_sum[slot, i, h] = route_gram(slot, tgx[2 * i + h], 2 + 2 * i + h, panels).astype(BF)
+            give_back(slot, i).start()
+
+    def add_scores(some):
+        rows16 = lax.broadcasted_iota(jnp.int32, (16, TOK), 0).astype(F32)
+        classes = lane.astype(F32)
+        owners, values = [], ([], [])
+        for slot in some:
+            owners.append((slots[slot, 0].astype(F32)[:, TOP : TOP + 1] == classes).astype(BF))
+            for i in range(2):
+                give_back(slot, i).wait_recv()
+            for h in range(2):
+                back = back_sum[slot, 0, h].astype(F32) + back_sum[slot, 1, h].astype(F32)
+                values[h].append((near_sum[slot, h] + back) * xs[slot, h])
+        owners = jnp.concatenate(owners, axis=0)
+        sums = []
         for h in range(2):
-            panels = range(i * GP // 2, (i + 1) * GP // 2)
-            far_sum[pair, i, h] = route_gram(pair, tgx[2 * i + h], 2 + 2 * i + h, panels).astype(BF)
-        give_back(pair, i).start()
+            hi, lo = split(jnp.concatenate(values[h], axis=0))
+            examples = (rows16 == marks[h, TOP : TOP + 1, :]).astype(BF)
+            sums.append((nt(examples, hi) + nt(examples, lo))[0:8, :])
+        hi, lo = split(jnp.concatenate(sums, axis=0))
+        part = jnp.dot(hi, owners, preferred_element_type=F32)
+        acc[...] += part + jnp.dot(lo, owners, preferred_element_type=F32)
 
     def taken(j):
         return (core == 0) | (j >= 1)
@@ -299,10 +314,6 @@
     @pl.loop(0, SLOTS + LAG)
     def _(j):
         fresh = (j < SLOTS) & taken(j)
-        ready = j >= LAG
-        since = jnp.maximum(j - LAG, 0)
-        pair = since // 2
-        at_home = (since % 2 == 0) != (pair == PAIRS - 1)
 
         def pass_on(part):
             @pl.when(fresh)
@@ -318,19 +329,7 @@
                     ring(j, part, 1).start()
 
         pass_on(0)
-
-        @pl.when(j == LAG + 1)
-        def _():
-            swaps[9].wait_recv()
-            swaps[10].wait_recv()
-
-        pl.when(ready & at_home)(lambda: feature_gram(pair))
-        pl.when(ready & ~at_home)(lambda: mate_tokens(pair, 0))
         pass_on(1)
-        pl.when(ready & at_home)(lambda: own_tokens(pair))
-        pl.when(ready & ~at_home)(lambda: mate_tokens(pair, 1))
-        pass_on(2)
-        pl.when(j == LAG - 1)(meet_core)
 
         @pl.when((j >= 1) & (j < SLOTS + 1) & taken(j - 1))
         def _():
@@ -340,7 +339,10 @@
                     ring(slot, axis, kind, True).wait_recv()
                     ring(slot, axis, kind + 2).start()
 
-        pl.when(j == LAG)(meet_mates)
+        pl.when(j == 0)(give_core_grad)
+        pl.when(j == 1)(give_core_x)
+        pl.when(j == LAG)(meet_core)
+        pl.when(j == SLOTS + LAG - 1)(lambda: add_scores(range(SLOTS - 1)))
 
         @pl.when((j >= 2) & (j < SLOTS + 2) & taken(j - 2))
         def _():
@@ -349,27 +351,23 @@
                 for axis in range(2):
                     ring(slot, axis, kind, True).wait_recv()
 
-    rows = lax.broadcasted_iota(jnp.int32, (LANE, LANE), 0).astype(F32)
-    rows16 = lax.broadcasted_iota(jnp.int32, (16, TOK), 0).astype(F32)
-    owners, values = [], ([], [])
-    for pair in range(PAIRS):
-        info = [slots[2 * pair + i, 0, 0:16, :].astype(F32) for i in range(2)]
-        info = jnp.where(lane < PROW, info[0], info[1])
-        owners.append((rows == info[TOP : TOP + 1, :]).astype(BF))
-        for i in range(2):
-            give_back(pair, i).wait_recv()
-        for h in range(2):
-            back = back_sum[pair, 0, h].astype(F32) + back_sum[pair, 1, h].astype(F32)
-            values[h].append((near_sum[pair, h] + back) * xs[pair, h])
-    owners = jnp.concatenate(owners, axis=1)
-    sums = []
-    for h in range(2):
-        hi, lo = split(jnp.concatenate(values[h], axis=1))
-        examples = (rows16 == marks[h, TOP : TOP + 1, :]).astype(BF)
-        part = jnp.dot(examples, hi, preferred_element_type=F32) + jnp.dot(examples, lo, preferred_element_type=F32)
-        sums.append(part[0:8, :])
-    hi, lo = split(jnp.concatenate(sums, axis=0))
-    acc[...] = nt(hi, owners) + nt(lo, owners)
+        @pl.when(j >= MEET)
+        def _():
+            @pl.when(j == MEET)
+            def _():
+                swaps[9].wait_recv()
+                swaps[10].wait_recv()
+
+            late = 2 * (j - MEET)
+            begin = jnp.minimum(late, j - LAG)
+            end = jnp.minimum(late + 2, j - LAG + 1)
+            pl.loop(begin, end)(mate_tokens)
+
+        pass_on(2)
+        pl.when(j >= LAG)(lambda: own_tokens(jnp.maximum(j - LAG, 0)))
+        pl.when(j == MEET - 1)(meet_mates)
+
+    add_scores([SLOTS - 1])
 
     last = swap(acc.at[pl.ds(8, 8)], rbuf, 11, other)
     last.start()
@@ -380,10 +378,10 @@
     for copy in swaps:
         copy.wait_send()
 
-    @pl.loop(0, PAIRS)
-    def _(pair):
+    @pl.loop(0, SLOTS)
+    def _(slot):
         for i in range(2):
-            give_back(pair, i).wait_send()
+            give_back(slot, i).wait_send()
 
     @pl.loop(0, SLOTS)
     def _(j):
@@ -418,19 +416,20 @@
         out_specs=vmem,
         scratch_shapes=[
             pltpu.VMEM((SLOTS + 1, PANELS, PROW, LANE), BF),
-            pltpu.VMEM((2, TOK, D), BF),
-            pltpu.VMEM((2, TOP, TOK, KH), BF),
-            pltpu.VMEM((4, TOP, TOK, KQ), BF),
+            pltpu.VMEM((2, D, TOK), BF),
+            pltpu.VMEM((2, KH, TOP * TOK), BF),
+            pltpu.VMEM((4, KQ, TOP * TOK), BF),
+            pltpu.VMEM((2, KQ, TOP * TOK), BF),
+            pltpu.VMEM((TOK, D), BF),
+            pltpu.VMEM((TOP, TOK, KH), BF),
             pltpu.VMEM((2, TOP, TOK, KQ), BF),
             pltpu.VMEM((TOP, PROW, KH), BF),
-            pltpu.VMEM((6, TOP, TOK, LANE), F32),
             pltpu.VMEM((6, 16, LANE), F32),
             pltpu.VMEM((LANE, LANE), F32),
-            pltpu.VMEM((PROW, LANE), F32),
-            pltpu.VMEM((PAIRS, 2, TOK, LANE), F32),
-            pltpu.VMEM((PAIRS, 2, TOK, LANE), F32),
-            pltpu.VMEM((PAIRS, 2, 2, TOK, LANE), BF),
-            pltpu.VMEM((PAIRS, 2, 2, TOK, LANE), BF),
+            pltpu.VMEM((SLOTS, 2, PROW, LANE), F32),
+            pltpu.VMEM((SLOTS, 2, PROW, LANE), F32),
+            pltpu.VMEM((SLOTS, 2, 2, PROW, LANE), BF),
+            pltpu.VMEM((SLOTS, 2, 2, PROW, LANE), BF),
             pltpu.VMEM((16, LANE), F32),
             pltpu.VMEM((8, LANE), F32),
             dma((8,)),
@@ -440,8 +439,8 @@
             dma((SLOTS, 2, 4)),
             dma((12,)),
             dma((12,)),
-            dma((PAIRS, 2)),
-            dma((PAIRS, 2)),
+            dma((SLOTS, 2)),
+            dma((SLOTS, 2)),
         ],
         compiler_params=pltpu.CompilerParams(
             collective_id=0, has_side_effects=True, vmem_limit_bytes=56 * 1024 * 1024

time: 82 us -> 94.6 us (1.15)
  Pallas kernels: 80.6 us -> 93.1 us
    pallas_call x1, Pallas kernels: 80.6 us -> 93.1 us  [body(): pl.pallas_call(kernel, out_shape=jax.ShapeDtypeStruct((EX_DEV, LANE), F32...]
where the time goes in v7:
time: 94.6 us; the launch traced here: 94.4 us
  Pallas kernels  93.1 us (98%)
  local copies, waits for them, and re-layouts  1.26 us (1%)
    pallas_call x1, Pallas kernels, body(): pl.pallas_call(kernel, out_shape=jax.ShapeDtypeStruct((EX_DEV, LANE), F32...  93.1 us

profile of v7, /device:TPU:1, one launch (start us, length us, event | category | flops | bytes accessed | tf_op | source)
XLA Modules:
  0.0 94.4 jit_solution(12173731379691802196)
XLA Ops:
  0.0 93.1 %ghost_scores.1 = f32[4,128]{1,0:T(4,128)} custom-call(bf16[128,5120]{1,0:T(8,128)(2,1)} %tx_hbm.1, bf16[6,128,1536]{2,1,0:T(8,128)(2,1)} %bitcast.8, s32[6,128]{1,0:T(8,128)} %bitcast.10, f32[6,128]{1,0:T(8,128)} %bitcast.11, s32[1,128]{1,0:T(1,128)} %bitcast.14, bf16[64,5120]{1,0:T(8,128)(2,1)} %px_hbm.1, bf16[6,64,1536]{2,1,0:T(8,128)(2,1)} %bitcast.9, ...), custom_call_target="tpu_custom_call" | custom-call | flops 16000000000 | bytes 6000000 | tf_op jit(solution)/shard_map/ghost_scores/pallas_call | solution.py:412
  93.1 1.3 %copy.12 = f32[4,128]{1,0:T(4,128)} copy(f32[4,128]{1,0:T(4,128)} %ghost_scores.1) | data formatting | bytes 4096

commit v8 on v5

--- a/solution.py
+++ b/solution.py
@@ -33,7 +33,6 @@
 PARTS = (10, 6)
 BASES = (PANELS - NR * PARTS[0], PANELS - NR * sum(PARTS))
 PAIRS = SLOTS // 2
-LAG = 4
 
 
 def nt(a, b):
@@ -254,10 +253,11 @@
             spread(group)
 
     def feature_gram(pair):
-        px = jnp.concatenate(
-            [jnp.concatenate([slots[2 * pair + i, X0 + c] for c in range(XP)], axis=1) for i in range(2)], axis=0
-        )
-        xs[pair] = nt(tx[...].reshape(2 * TOK, D), px).reshape(2, TOK, LANE)
+        px = [jnp.concatenate([slots[2 * pair - 2 + i, X0 + c] for c in range(XP)], axis=1) for i in range(4)]
+        gram = nt(tx[...].reshape(2 * TOK, D), jnp.concatenate(px, axis=0))
+        for i in range(2):
+            for h in range(2):
+                xs[pair - 1 + i, h] = gram[h * TOK : (h + 1) * TOK, i * LANE : (i + 1) * LANE]
 
     def route_gram(pair, lhs, group, panels):
         info = [slots[2 * pair + i, 0, 0:16, :].astype(F32) for i in range(2)]
@@ -271,41 +271,44 @@
             ],
             axis=1,
         )
-        gram = nt(lhs.reshape(TOP * TOK, len(panels) * LANE), pg)
-        total = jnp.zeros((TOK, LANE), F32)
-        for r in range(TOP):
-            who = ids[group, r]
-            for q in range(TOP):
-                part = gram[r * TOK : (r + 1) * TOK, q * LANE : (q + 1) * LANE]
-                total = total + jnp.where(who == info[q : q + 1, :], part, 0.0)
-        return total
+        gram = nt(lhs.reshape(2 * TOP * TOK, len(panels) * LANE), pg)
+        sums = []
+        for h in range(2):
+            total = jnp.zeros((TOK, LANE), F32)
+            for r in range(TOP):
+                who = ids[group + h, r]
+                row = (h * TOP + r) * TOK
+                for q in range(TOP):
+                    part = gram[row : row + TOK, q * LANE : (q + 1) * LANE]
+                    total = total + jnp.where(who == info[q : q + 1, :], part, 0.0)
+            sums.append(total)
+        return sums
 
     def give_back(pair, i):
         return remote(far_sum.at[pair, i], back_sum.at[pair, i], qs.at[pair, i], qr.at[pair, i], mates[i])
 
     def own_tokens(pair):
-        for h in range(2):
-            near_sum[pair, h] = route_gram(pair, tg[h], h, range(GP))
+        for h, total in enumerate(route_gram(pair, tg[...], 0, range(GP))):
+            near_sum[pair, h] = total
 
     def mate_tokens(pair, i):
-        for h in range(2):
-            panels = range(i * GP // 2, (i + 1) * GP // 2)
-            far_sum[pair, i, h] = route_gram(pair, tgx[2 * i + h], 2 + 2 * i + h, panels).astype(BF)
+        panels = range(i * GP // 2, (i + 1) * GP // 2)
+        for h, total in enumerate(route_gram(pair, tgx[2 * i : 2 * i + 2], 2 + 2 * i, panels)):
+            far_sum[pair, i, h] = total.astype(BF)
         give_back(pair, i).start()
 
     def taken(j):
         return (core == 0) | (j >= 1)
 
-    @pl.loop(0, SLOTS + LAG)
+    @pl.loop(0, SLOTS + 3)
     def _(j):
-        fresh = (j < SLOTS) & taken(j)
-        ready = j >= LAG
-        since = jnp.maximum(j - LAG, 0)
-        pair = since // 2
-        at_home = (since % 2 == 0) != (pair == PAIRS - 1)
+        odd_step = j % 2 == 1
+        home = ((j >= 3) & (j < SLOTS) & odd_step) | (j == SLOTS + 2)
+        visit = ((j >= 4) & (j <= SLOTS) & ~odd_step) | (j == SLOTS + 1)
+        pair = jnp.clip((j - 3) // 2, 0, PAIRS - 1)
 
         def pass_on(part):
-            @pl.when(fresh)
+            @pl.when((j < SLOTS) & taken(j))
             def _():
                 zcopy(j, j, part).wait_recv()
 
@@ -318,36 +321,35 @@
                     ring(j, part, 1).start()
 
         pass_on(0)
-
-        @pl.when(j == LAG + 1)
-        def _():
-            swaps[9].wait_recv()
-            swaps[10].wait_recv()
-
-        pl.when(ready & at_home)(lambda: feature_gram(pair))
-        pl.when(ready & ~at_home)(lambda: mate_tokens(pair, 0))
         pass_on(1)
-        pl.when(ready & at_home)(lambda: own_tokens(pair))
-        pl.when(ready & ~at_home)(lambda: mate_tokens(pair, 1))
-        pass_on(2)
-        pl.when(j == LAG - 1)(meet_core)
 
         @pl.when((j >= 1) & (j < SLOTS + 1) & taken(j - 1))
         def _():
-            slot = jnp.maximum(j - 1, 0)
+            slot = jnp.clip(j - 1, 0, SLOTS - 1)
             for kind in range(2):
                 for axis in range(2):
                     ring(slot, axis, kind, True).wait_recv()
                     ring(slot, axis, kind + 2).start()
 
-        pl.when(j == LAG)(meet_mates)
-
         @pl.when((j >= 2) & (j < SLOTS + 2) & taken(j - 2))
         def _():
-            slot = jnp.maximum(j - 2, 0)
+            slot = jnp.clip(j - 2, 0, SLOTS - 1)
             for kind in range(2, 4):
                 for axis in range(2):
                     ring(slot, axis, kind, True).wait_recv()
+
+        @pl.when(j == 4)
+        def _():
+            swaps[9].wait_recv()
+            swaps[10].wait_recv()
+
+        pl.when(home)(lambda: own_tokens(pair))
+        pl.when(visit)(lambda: mate_tokens(pair, 0))
+        pass_on(2)
+        pl.when(visit)(lambda: mate_tokens(pair, 1))
+        pl.when((j == 6) | (j == SLOTS + 2))(lambda: feature_gram(jnp.where(j == 6, 1, PAIRS - 1)))
+        pl.when(j == 2)(meet_core)
+        pl.when(j == 3)(meet_mates)
 
     rows = lax.broadcasted_iota(jnp.int32, (LANE, LANE), 0).astype(F32)
     rows16 = lax.broadcasted_iota(jnp.int32, (16, TOK), 0).astype(F32)

time: 82 us -> 83.4 us (1.017)
  Pallas kernels: 80.6 us -> 81.9 us
    pallas_call x1, Pallas kernels: 80.6 us -> 81.9 us  [body(): pl.pallas_call(kernel, out_shape=jax.ShapeDtypeStruct((EX_DEV, LANE), F32...]
where the time goes in v8:
time: 83.4 us; the launch traced here: 83.2 us
  Pallas kernels  81.9 us (98%)
  local copies, waits for them, and re-layouts  1.26 us (2%)
    pallas_call x1, Pallas kernels, body(): pl.pallas_call(kernel, out_shape=jax.ShapeDtypeStruct((EX_DEV, LANE), F32...  81.9 us

profile of v8, /device:TPU:1, one launch (start us, length us, event | category | flops | bytes accessed | tf_op | source)
XLA Modules:
  0.0 83.2 jit_solution(1388717250551871568)
XLA Ops:
  0.0 81.9 %ghost_scores.1 = f32[4,128]{1,0:T(4,128)} custom-call(bf16[128,5120]{1,0:T(8,128)(2,1)} %tx_hbm.1, bf16[6,128,1536]{2,1,0:T(8,128)(2,1)} %bitcast.8, s32[6,128]{1,0:T(8,128)} %bitcast.10, f32[6,128]{1,0:T(8,128)} %bitcast.11, s32[1,128]{1,0:T(1,128)} %bitcast.14, bf16[64,5120]{1,0:T(8,128)(2,1)} %px_hbm.1, bf16[6,64,1536]{2,1,0:T(8,128)(2,1)} %bitcast.9, ...), custom_call_target="tpu_custom_call" | custom-call | flops 16000000000 | bytes 6000000 | tf_op jit(solution)/shard_map/ghost_scores/pallas_call | solution.py:416
  81.9 1.3 %copy.12 = f32[4,128]{1,0:T(4,128)} copy(f32[4,128]{1,0:T(4,128)} %ghost_scores.1) | data formatting | bytes 4096

commit v9 on v5

--- a/solution.py
+++ b/solution.py
@@ -254,10 +254,11 @@
             spread(group)
 
     def feature_gram(pair):
-        px = jnp.concatenate(
-            [jnp.concatenate([slots[2 * pair + i, X0 + c] for c in range(XP)], axis=1) for i in range(2)], axis=0
-        )
-        xs[pair] = nt(tx[...].reshape(2 * TOK, D), px).reshape(2, TOK, LANE)
+        px = [jnp.concatenate([slots[2 * pair - 2 + i, X0 + c] for c in range(XP)], axis=1) for i in range(4)]
+        gram = nt(tx[...].reshape(2 * TOK, D), jnp.concatenate(px, axis=0))
+        for i in range(2):
+            for h in range(2):
+                xs[pair - 1 + i, h] = gram[h * TOK : (h + 1) * TOK, i * LANE : (i + 1) * LANE]
 
     def route_gram(pair, lhs, group, panels):
         info = [slots[2 * pair + i, 0, 0:16, :].astype(F32) for i in range(2)]
@@ -317,14 +318,22 @@
                     ring(j, part, 0).start()
                     ring(j, part, 1).start()
 
+        def hop():
+            slot = jnp.clip(j - 1, 0, SLOTS - 1)
+            for kind in range(2):
+                for axis in range(2):
+                    ring(slot, axis, kind, True).wait_recv()
+                    ring(slot, axis, kind + 2).start()
+
         pass_on(0)
+        pl.when(j == SLOTS)(hop)
 
         @pl.when(j == LAG + 1)
         def _():
             swaps[9].wait_recv()
             swaps[10].wait_recv()
 
-        pl.when(ready & at_home)(lambda: feature_gram(pair))
+        pl.when(ready & at_home & (pair % 2 == 1))(lambda: feature_gram(jnp.maximum(pair, 1)))
         pl.when(ready & ~at_home)(lambda: mate_tokens(pair, 0))
         pass_on(1)
         pl.when(ready & at_home)(lambda: own_tokens(pair))
@@ -332,13 +341,7 @@
         pass_on(2)
         pl.when(j == LAG - 1)(meet_core)
 
-        @pl.when((j >= 1) & (j < SLOTS + 1) & taken(j - 1))
-        def _():
-            slot = jnp.maximum(j - 1, 0)
-            for kind in range(2):
-                for axis in range(2):
-                    ring(slot, axis, kind, True).wait_recv()
-                    ring(slot, axis, kind + 2).start()
+        pl.when((j >= 1) & (j < SLOTS) & taken(j - 1))(hop)
 
         pl.when(j == LAG)(meet_mates)
 

time: 82 us -> 82.1 us (level)
  no operation moved by 1% of the time
where the time goes in v9:
time: 82.1 us; the launch traced here: 81.9 us
  Pallas kernels  80.7 us (98%)
  local copies, waits for them, and re-layouts  1.26 us (2%)
    pallas_call x1, Pallas kernels, body(): pl.pallas_call(kernel, out_shape=jax.ShapeDtypeStruct((EX_DEV, LANE), F32...  80.7 us

profile of v9, /device:TPU:1, one launch (start us, length us, event | category | flops | bytes accessed | tf_op | source)
XLA Modules:
  0.0 81.9 jit_solution(8578311450624480174)
XLA Ops:
  0.0 80.7 %ghost_scores.1 = f32[4,128]{1,0:T(4,128)} custom-call(bf16[128,5120]{1,0:T(8,128)(2,1)} %tx_hbm.1, bf16[6,128,1536]{2,1,0:T(8,128)(2,1)} %bitcast.8, s32[6,128]{1,0:T(8,128)} %bitcast.10, f32[6,128]{1,0:T(8,128)} %bitcast.11, s32[1,128]{1,0:T(1,128)} %bitcast.14, bf16[64,5120]{1,0:T(8,128)(2,1)} %px_hbm.1, bf16[6,64,1536]{2,1,0:T(8,128)(2,1)} %bitcast.9, ...), custom_call_target="tpu_custom_call" | custom-call | flops 16000000000 | bytes 6000000 | tf_op jit(solution)/shard_map/ghost_scores/pallas_call | solution.py:417
  80.7 1.3 %copy.12 = f32[4,128]{1,0:T(4,128)} copy(f32[4,128]{1,0:T(4,128)} %ghost_scores.1) | data formatting | bytes 4096

commit v10 on v9

--- a/solution.py
+++ b/solution.py
@@ -30,7 +30,7 @@
 X0 = 1
 G0 = X0 + XP
 PANELS = G0 + GP * TOP
-PARTS = (10, 6)
+PARTS = (11, 7)
 BASES = (PANELS - NR * PARTS[0], PANELS - NR * sum(PARTS))
 PAIRS = SLOTS // 2
 LAG = 4

time: 82.1 us -> 85.3 us (1.039)
  Pallas kernels: 80.7 us -> 83.9 us
    pallas_call x1, Pallas kernels: 80.7 us -> 83.9 us  [body(): pl.pallas_call(kernel, out_shape=jax.ShapeDtypeStruct((EX_DEV, LANE), F32...]
where the time goes in v10:
time: 85.3 us; the launch traced here: 85.1 us
  Pallas kernels  83.9 us (98%)
  local copies, waits for them, and re-layouts  1.26 us (1%)
    pallas_call x1, Pallas kernels, body(): pl.pallas_call(kernel, out_shape=jax.ShapeDtypeStruct((EX_DEV, LANE), F32...  83.9 us

profile of v10, /device:TPU:1, one launch (start us, length us, event | category | flops | bytes accessed | tf_op | source)
XLA Modules:
  0.0 85.1 jit_solution(16916249202880494601)
XLA Ops:
  0.0 83.9 %ghost_scores.1 = f32[4,128]{1,0:T(4,128)} custom-call(bf16[128,5120]{1,0:T(8,128)(2,1)} %tx_hbm.1, bf16[6,128,1536]{2,1,0:T(8,128)(2,1)} %bitcast.8, s32[6,128]{1,0:T(8,128)} %bitcast.10, f32[6,128]{1,0:T(8,128)} %bitcast.11, s32[1,128]{1,0:T(1,128)} %bitcast.14, bf16[64,5120]{1,0:T(8,128)(2,1)} %px_hbm.1, bf16[6,64,1536]{2,1,0:T(8,128)(2,1)} %bitcast.9, ...), custom_call_target="tpu_custom_call" | custom-call | flops 16000000000 | bytes 6000000 | tf_op jit(solution)/shard_map/ghost_scores/pallas_call | solution.py:417
  83.9 1.3 %copy.12 = f32[4,128]{1,0:T(4,128)} copy(f32[4,128]{1,0:T(4,128)} %ghost_scores.1) | data formatting | bytes 4096
